TPU v7x, 32 devices: a whole 2x2x4 slice. The times are simulated.
32 devices in a mesh: rep: 2 (over x), pg: 16 (over z, y, core).
Axes of the slice: x: 2, y: 2, z: 4, core: 2. Of those that a mesh axis runs over, the one named last changes fastest.
Arguments:
- queries: bfloat16 [32, 128, 4096], P(('rep', 'pg')), parts along dimension 0, may hold values from -6 to 6
- block_kv: bfloat16 [32, 128, 1024], P(('rep', 'pg')), parts along dimension 0, may hold values from -6 to 6
- pool_kv: bfloat16 [32, 16, 32, 1024], P(('rep', 'pg')), parts along dimension 0, may hold values from -6 to 6
- prefix_len: int32 [32], P('rep'), parts along dimension 0, may hold values from 0 to 512, as said below
- assignment: int32 [32], P('rep'), parts along dimension 0, may hold values from 0 to 15, each once
- stripe_map: int32 [32, 16], P('rep'), parts along dimension 0, may hold values from 0 to 15, each once within a row
- owner_map: int32 [32, 16], P('rep'), parts along dimension 0, may hold values from 0 to 15, each once within a row
Outputs:
- attended: bfloat16 [32, 128, 4096], P(('rep', 'pg')), parts along dimension 0
- decode_kv: bfloat16 [32, 16, 8, 1024], P(('rep', 'pg')), parts along dimension 0
There are 2 independent parts, one for each index of `rep`. A program takes and returns all parts, laid end to end along the dimension named above; each array names one. Nothing has to cross between parts.
Inputs may be any that keep to these rules, and one draw needn't show every extreme that they name: `prefix_len`: some request has exactly 512. `assignment`: each group computes a different request. `stripe_map`: each row names every device once. `owner_map`: each row names every device once.
All inputs are finite; a program needn't handle non-finite values.
Results may differ from a plain program's by a relative error of at most 0.0079.
Values may be sent and summed in bfloat16 or wider, within the bound.
No kernel may reach another device: no remote copies, remote signals or barrier semaphores. Data moves between devices by JAX's collectives and lax.ppermute only.
A program may use at most 64 MiB of HBM per device.

v0:
```python
import jax
import jax.numpy as jnp
from jax import lax
from jax.sharding import PartitionSpec as P

Q_HEADS = 32
KV_HEADS = 4


ROPE_BASE = 1000000.0
MASKED = -1e30


def invert(table):
    count = table.shape[-1]
    places = jnp.arange(count, dtype=jnp.int32)
    hits = table[..., None, :] == places[:, None]
    return jnp.sum(jnp.where(hits, places, 0), axis=-1)


def rotate(rows, positions, heads):
    head_width = rows.shape[-1] // heads
    half_width = head_width // 2
    freqs = ROPE_BASE ** (-jnp.arange(half_width, dtype=jnp.float32) / half_width)
    angles = positions.astype(jnp.float32)[:, None] * freqs[None, :]
    cosine = jnp.concatenate([jnp.cos(angles), jnp.cos(angles)], axis=-1)[:, None, :]
    sine = jnp.concatenate([jnp.sin(angles), jnp.sin(angles)], axis=-1)[:, None, :]
    split_rows = rows.astype(jnp.float32).reshape(rows.shape[0], heads, head_width)
    turned = jnp.concatenate([-split_rows[..., half_width:], split_rows[..., :half_width]], axis=-1)
    return (split_rows * cosine + turned * sine).reshape(rows.shape).astype(jnp.bfloat16)


def absorb(carried, query_heads, block_rows, live):
    kv_width = block_rows.shape[-1] // 2
    head_count = query_heads.shape[0]
    head_width = query_heads.shape[-1]
    key_rows = block_rows[:, :kv_width].reshape(-1, head_count, head_width)
    value_rows = block_rows[:, kv_width:].reshape(-1, head_count, head_width)
    scores = jnp.einsum(
        "hqd,khd->hqk", query_heads, key_rows, preferred_element_type=jnp.float32
    ) / jnp.sqrt(jnp.float32(head_width))
    scores = jnp.where(live[None], scores, MASKED)
    old_high, old_total, old_sums = carried
    new_high = jnp.maximum(old_high, jnp.max(scores, axis=-1))
    weights = jnp.where(live[None], jnp.exp(scores - new_high[..., None]), 0.0)
    factor = jnp.exp(old_high - new_high)
    new_total = old_total * factor + jnp.sum(weights, axis=-1)
    new_sums = old_sums * factor[..., None] + jnp.einsum(
        "hqk,khd->hqd", weights.astype(jnp.bfloat16), value_rows, preferred_element_type=jnp.float32
    )
    return (new_high, new_total, new_sums)


def block_width():
    return 512


def sweep_keys(carried, query_heads, key_list, live_list, block_total):

    def visit(index, running):
        return absorb(running, query_heads, key_list, live_list[None, :])

    return lax.fori_loop(0, block_total, visit, carried)


def shards(queries, block_kv, pool_kv, prefix_len, assignment, stripe_map, owner_map):
    groups = lax.axis_size("pg")
    myself = lax.axis_index("pg")
    new_count = queries.shape[1]
    kv_width = block_kv.shape[2] // 2
    slot_count = pool_kv.shape[2]
    prefix_span = slot_count * groups
    request = assignment[myself]
    length = prefix_len[request]
    offsets = jnp.arange(new_count, dtype=jnp.int32)
    positions = length + offsets
    q_rot = rotate(queries[0], positions, Q_HEADS)
    new_kv = jnp.concatenate(
        [rotate(block_kv[0, :, :kv_width], positions, KV_HEADS), block_kv[0, :, kv_width:]], axis=1
    )
    targets = invert(owner_map[request])
    spread = jnp.transpose(new_kv.reshape(new_count // groups, groups, 2 * kv_width), (1, 0, 2))
    fresh_out = spread[targets]
    local_pool = pool_kv[0]
    outgoing = local_pool[assignment]
    arrived = lax.all_to_all(fresh_out, "pg", split_axis=0, concat_axis=0, tiled=True)
    incoming = lax.all_to_all(outgoing, "pg", split_axis=0, concat_axis=0, tiled=True)
    decode_kv = arrived[invert(assignment)][None]
    per_group = Q_HEADS // KV_HEADS
    head_width = q_rot.shape[1] // Q_HEADS
    query_heads = jnp.transpose(
        q_rot.reshape(new_count, KV_HEADS, per_group, head_width), (1, 2, 0, 3)
    ).reshape(KV_HEADS, per_group * new_count, head_width)
    causal = offsets[None, :] <= jnp.tile(offsets, per_group)[:, None]
    blank = (
        jnp.full((KV_HEADS, per_group * new_count), MASKED, jnp.float32),
        jnp.zeros((KV_HEADS, per_group * new_count), jnp.float32),
        jnp.zeros((KV_HEADS, per_group * new_count, head_width), jnp.float32),
    )
    carried = absorb(blank, query_heads, new_kv, causal)
    residues = invert(stripe_map[request])
    located = jnp.arange(slot_count, dtype=jnp.int32)[None, :] * groups + residues[:, None]
    live_list = (located < length).reshape(-1)
    key_list = incoming.reshape(prefix_span, 2 * kv_width)
    key_block = block_width()
    carried = sweep_keys(carried, query_heads, key_list, live_list, prefix_span // key_block)
    highest, totals, sums = carried
    result = (sums / totals[..., None]).reshape(KV_HEADS, per_group, new_count, head_width)
    attended = (
        jnp.transpose(result, (2, 0, 1, 3))
        .reshape(new_count, Q_HEADS * head_width)
        .astype(jnp.bfloat16)
    )
    return (attended[None], decode_kv)


def solution(mesh):
    return jax.shard_map(
        shards,
        mesh=mesh,
        in_specs=(
            P(("rep", "pg"), None, None),
            P(("rep", "pg"), None, None),
            P(("rep", "pg"), None, None, None),
            P("rep"),
            P("rep"),
            P("rep", None),
            P("rep", None),
        ),
        out_specs=(P(("rep", "pg"), None, None), P(("rep", "pg"), None, None, None)),
        check_vma=False,
    )
```

profile of v0, /device:TPU:11, one launch (start us, length us, event | category | flops | bytes accessed | tf_op | source)
XLA Modules:
  0.0 72.4 jit_solution(10576154855994704719)
XLA Ops:
  0.6 1.3 %dynamic_slice.12 = s32[1]{0:T(128)} dynamic-slice(s32[16]{0:T(128)} %param.11, s32[]{:T(128)S(6)} %select_n.57), dynamic_slice_sizes={1} | dynamic-slice | bytes 12 | tf_op jit(solution)/shard_map/dynamic_slice | solution.py:73
  3.9 1.2 %dynamic_slice.13 = s32[1]{0:T(128)} dynamic-slice(s32[16]{0:T(128)} %param.10, s32[]{:T(128)S(6)} %select_n.58), dynamic_slice_sizes={1} | dynamic-slice | bytes 12 | tf_op jit(solution)/shard_map/dynamic_slice | solution.py:74
  7.3 1.0 %fusion.32 = (bf16[1,128,512]{2,1,0:T(8,128)(2,1)S(1)}, f32[1,128,512]{2,1,0:T(8,128)S(1)}) fusion(bf16[1,128,1024]{2,1,0:T(8,128)(2,1)} %param.8), kind=kLoop, calls=%fused_computation.76 | loop fusion | flops 65536 | bytes 655360 | tf_op jit(solution)/shard_map/slice | solution.py:79
  8.7 0.9 %add_convert_fusion = (bf16[128,4,128]{2,1,0:T(4,128)(2,1)}, f32[128,4,128]{2,1,0:T(4,128)S(1)}) fusion(f32[128,4,128]{2,1,0:T(4,128)S(1)} %reshape.190, f32[128,128]{1,0:T(8,128)S(1)} %get-tuple-element.46, f32[128,128]{1,0:T(8,128)S(1)} %get-tuple-element.47, f32[128,4,64]{2,1,0:T(4,128)S(1)} %get-tuple-element.34, f32[128,4,64]{2,1,0:T(4,128)S(1)} %get-tuple-element.33), kind=kLoop, calls=%fused_computation.35 | loop fusion | flops 327680 | bytes 1048576 | tf_op jit(solution)/shard_map/convert_element_type | solution.py:30
  10.1 1.3 %gather_fusion.1 = bf16[16,8,1024]{2,1,0:T(8,128)(2,1)} fusion(bf16[16,8,1024]{2,1,0:T(8,128)(2,1)S(1)} %maximum_bitcast_fusion.1, s32[1024]{0:T(1024)S(1)} %pad_clamp_fusion.1), kind=kCustom, calls=%fused_computation.1 | custom fusion | bytes 524352 | tf_op jit(solution)/shard_map/gather | solution.py:83
  11.4 6.6 %all-to-all-start.1 = ((bf16[16,8,1024]{2,1,0:T(8,128)(2,1)}), bf16[16,8,1024]{2,1,0:T(8,128)(2,1)S(1)}, u32[]{:S(2)}, u32[]{:S(2)}) async-start(bf16[16,8,1024]{2,1,0:T(8,128)(2,1)} %gather_fusion.1), calls=%async_computation.1 | async-start | bytes 524288 | tf_op jit(solution)/shard_map/all_to_all | solution.py:86
  18.0 0.7 %copy.65 = bf16[1,128,512]{1,2,0:T(8,128)(2,1)} copy(bf16[1,128,512]{2,1,0:T(8,128)(2,1)S(1)} %get-tuple-element.31) | data formatting | bytes 262144
  18.9 0.7 add_compare_fusion
  20.3 1.6 %gather_fusion = bf16[16,32,1024]{2,1,0:T(8,128)(2,1)} fusion(bf16[16,32,1024]{2,1,0:T(8,128)(2,1)S(1)} %bitcast.57, s32[1024]{0:T(1024)S(1)} %pad_clamp_fusion.2), kind=kCustom, calls=%fused_computation | custom fusion | bytes 2097216 | tf_op jit(solution)/shard_map/gather | solution.py:85
  21.9 4.8 %all-to-all-done.1 = bf16[16,8,1024]{2,1,0:T(8,128)(2,1)S(1)} async-done(((bf16[16,8,1024]{2,1,0:T(8,128)(2,1)}), bf16[16,8,1024]{2,1,0:T(8,128)(2,1)S(1)}, u32[]{:S(2)}, u32[]{:S(2)}) %all-to-all-start.1) | async-done | bytes 262176 | tf_op jit(solution)/shard_map/all_to_all | solution.py:86
  26.7 4.9 %all-to-all-start = ((bf16[16,32,1024]{2,1,0:T(8,128)(2,1)}), bf16[16,32,1024]{2,1,0:T(8,128)(2,1)S(1)}, u32[]{:S(2)}, u32[]{:S(2)}) async-start(bf16[16,32,1024]{2,1,0:T(8,128)(2,1)} %gather_fusion), calls=%async_computation | async-start | bytes 2097152 | tf_op jit(solution)/shard_map/all_to_all | solution.py:87
  32.2 0.7 %slice_negate_fusion = (f32[128,32,64]{2,1,0:T(8,128)S(1)}, f32[128,32,64]{2,1,0:T(8,128)S(1)}) fusion(f32[128,32,128]{2,1,0:T(8,128)S(1)} %bitcast.58), kind=kLoop, calls=%fused_computation.10 | loop fusion | flops 262144 | bytes 4194304 | tf_op jit(solution)/shard_map/neg | solution.py:29
  33.0 0.8 %fusion.13 = bf16[4,8,128,128]{3,1,0,2:T(8,128)(2,1)S(1)} fusion(f32[128,32,64]{2,1,0:T(8,128)S(1)} %get-tuple-element.28, f32[128,32,64]{2,1,0:T(8,128)S(1)} %get-tuple-element.20, f32[128,4,8,128]{3,2,1,0:T(8,128)S(1)} %bitcast.59, f32[128,128]{1,0:T(8,128)S(1)} %get-tuple-element.47, f32[128,128]{1,0:T(8,128)S(1)} %get-tuple-element.46), kind=kLoop, calls=%fused_computation.22 | loop fusion | flops 2621440 | bytes 5373952 | tf_op jit(solution)/shard_map/transpose | solution.py:91
  35.2 1.9 %fusion.9 = (f32[4,1024]{1,0:T(4,128)S(1)}, f32[4,1024,128]{1,2,0:T(8,128)}) fusion(pred[1024,128]{0,1:T(8,128)(4,1)S(1)} %iota_compare_fusion, bf16[4,1024,128]{2,1,0:T(8,128)(2,1)S(1)} %bitcast.60, bf16[128,4,128]{2,1,0:T(4,128)(2,1)S(1)} %copy-done.3), kind=kOutput, calls=%fused_computation.19 | convolution fusion | flops 135786496 | bytes 3424256 | tf_op jit(solution)/shard_map/hqd,khd->hqk/dot_general | solution.py:39
  37.1 1.4 %gather_fusion.2 = bf16[16,8,1024]{2,1,0:T(8,128)(2,1)} fusion(bf16[16,8,1024]{2,1,0:T(8,128)(2,1)S(1)} %all-to-all-done.1, s32[1024]{0:T(1024)} %pad_clamp_fusion), kind=kCustom, calls=%fused_computation.2 | custom fusion | bytes 524352 | tf_op jit(solution)/shard_map/gather | solution.py:88
  38.5 18.0 %all-to-all-done = bf16[16,32,1024]{2,1,0:T(8,128)(2,1)S(1)} async-done(((bf16[16,32,1024]{2,1,0:T(8,128)(2,1)}), bf16[16,32,1024]{2,1,0:T(8,128)(2,1)S(1)}, u32[]{:S(2)}, u32[]{:S(2)}) %all-to-all-start) | async-done | bytes 1048608 | tf_op jit(solution)/shard_map/all_to_all | solution.py:87
  56.5 1.1 %fusion.31 = (bf16[512,512]{1,0:T(8,128)(2,1)}, bf16[512,512]{1,0:T(8,128)(2,1)}) fusion(bf16[512,1024]{1,0:T(8,128)(2,1)S(1)} %bitcast.62), kind=kLoop, calls=%fused_computation.75 | loop fusion | bytes 2097152 | tf_op jit(solution)/shard_map/while/body/eval_jaxpr/slice | solution.py:37
  57.6 1.3 %copy.49 = bf16[512,512]{0,1:T(8,128)(2,1)S(1)} copy(bf16[512,512]{1,0:T(8,128)(2,1)} %get-tuple-element.29) | data formatting | bytes 1048576 | tf_op jit(solution)/shard_map/while/body/eval_jaxpr/slice | solution.py:37
  58.8 1.3 %copy.51 = bf16[512,512]{0,1:T(8,128)(2,1)S(1)} copy(bf16[512,512]{1,0:T(8,128)(2,1)} %get-tuple-element.30) | data formatting | bytes 1048576 | tf_op jit(solution)/shard_map/while/body/eval_jaxpr/slice | solution.py:38
  60.1 1.7 %fusion = (f32[4,1024]{1,0:T(4,128)S(1)}, f32[4,1024,512]{1,2,0:T(8,128)S(1)}) fusion(pred[512]{0:T(512)(128)(4,1)S(1)} %copy-done.5, bf16[4,1024,128]{2,1,0:T(8,128)(2,1)S(1)} %bitcast.61, bf16[512,4,128]{0,2,1:T(8,128)(2,1)S(1)} %bitcast.64), kind=kOutput, calls=%fused_computation.5 | convolution fusion | flops 543158272 | bytes 9978368 | tf_op jit(solution)/shard_map/while/body/eval_jaxpr/hqd,khd->hqk/dot_general | solution.py:39
  61.8 2.3 %fusion.1 = f32[4,1024]{1,0:T(4,128)S(1)} fusion(f32[4,1024,512]{1,2,0:T(8,128)S(1)} %get-tuple-element.43, f32[4,1024]{1,0:T(4,128)S(1)} %get-tuple-element.36, pred[512]{0:T(512)(128)(4,1)S(1)} %copy-done.5), kind=kLoop, calls=%fused_computation.6 | loop fusion | flops 10481664 | bytes 8421888 | tf_op jit(solution)/shard_map/while/body/eval_jaxpr/reduce_sum | solution.py:47
  64.1 2.8 %fusion.3 = f32[4,1024,128]{2,1,0:T(8,128)S(1)} fusion(bf16[512,4,128]{0,2,1:T(8,128)(2,1)S(1)} %bitcast.67, f32[4,1024,512]{1,2,0:T(8,128)S(1)} %get-tuple-element.43, f32[4,1024]{1,0:T(4,128)S(1)} %get-tuple-element.36, pred[512]{0:T(512)(128)(4,1)S(1)} %copy-done.5), kind=kOutput, calls=%fused_computation.8 | convolution fusion | flops 547356672 | bytes 11026944 | tf_op jit(solution)/shard_map/while/body/eval_jaxpr/hqk,khd->hqd/dot_general | solution.py:48
  67.9 2.6 %divide_convert_fusion = bf16[4,1024,128]{2,1,0:T(8,128)(2,1)S(1)} fusion(f32[4,1024,128]{2,1,0:T(8,128)S(1)} %fusion.3, bf16[128,4,128]{0,2,1:T(8,128)(2,1)S(1)} %bitcast.69, f32[4,1024,128]{1,2,0:T(8,128)S(1)} %copy-done.1, f32[4,1024]{1,0:T(4,128)S(1)} %get-tuple-element.16, f32[4,1024]{1,0:T(4,128)S(1)} %get-tuple-element.17, ...), kind=kOutput, calls=%fused_computation.16 | convolution fusion | flops 139460608 | bytes 5570560 | tf_op jit(solution)/shard_map/hqk,khd->hqd/dot_general | solution.py:48
  71.1 1.3 %convert_element_type.88 = bf16[1,128,4096]{2,1,0:T(8,128)(2,1)} reshape(bf16[128,4,8,128]{3,2,1,0:T(8,128)(2,1)S(1)} %copy.54) | data formatting | bytes 2097152 | tf_op jit(solution)/shard_map/convert_element_type | solution.py:112
  (49 shorter events, 7.4 us)
Async XLA Ops:
  0.6 19.6 %copy-start = (bf16[1,16,32,1024]{3,2,1,0:T(8,128)(2,1)S(1)}, bf16[1,16,32,1024]{3,2,1,0:T(8,128)(2,1)}, u32[]{:S(2)}) copy-start(bf16[1,16,32,1024]{3,2,1,0:T(8,128)(2,1)} %param.9) | copy-start | bytes 3145732
  8.7 11.6 %copy-start.6 = (s32[16]{0:T(128)S(1)}, s32[16]{0:T(128)}, u32[]{:S(2)}) copy-start(s32[16]{0:T(128)} %param.11) | copy-start | bytes 196
  11.4 15.3 %all-to-all-start.1 = ((bf16[16,8,1024]{2,1,0:T(8,128)(2,1)}), bf16[16,8,1024]{2,1,0:T(8,128)(2,1)S(1)}, u32[]{:S(2)}, u32[]{:S(2)}) async-start(bf16[16,8,1024]{2,1,0:T(8,128)(2,1)} %gather_fusion.1), calls=%async_computation.1 | async-start | bytes 524288 | tf_op jit(solution)/shard_map/all_to_all | solution.py:86
  20.3 11.4 %copy-start.2 = (bf16[1,128,4096]{2,1,0:T(8,128)(2,1)S(1)}, bf16[1,128,4096]{2,1,0:T(8,128)(2,1)}, u32[]{:S(2)}) copy-start(bf16[1,128,4096]{2,1,0:T(8,128)(2,1)} %param.7) | copy-start | bytes 3145732
  26.7 29.8 %all-to-all-start = ((bf16[16,32,1024]{2,1,0:T(8,128)(2,1)}), bf16[16,32,1024]{2,1,0:T(8,128)(2,1)S(1)}, u32[]{:S(2)}, u32[]{:S(2)}) async-start(bf16[16,32,1024]{2,1,0:T(8,128)(2,1)} %gather_fusion), calls=%async_computation | async-start | bytes 2097152 | tf_op jit(solution)/shard_map/all_to_all | solution.py:87
  33.8 0.7 copy-start.7
  33.8 1.5 %copy-start.3 = (bf16[128,4,128]{2,1,0:T(4,128)(2,1)S(1)}, bf16[128,4,128]{2,1,0:T(4,128)(2,1)}, u32[]{:S(2)}) copy-start(bf16[128,4,128]{2,1,0:T(4,128)(2,1)} %get-tuple-element.18) | copy-start | bytes 393220
  56.5 3.6 %copy-start.5 = (pred[512]{0:T(512)(128)(4,1)S(1)}, pred[512]{0:T(512)(128)(4,1)}, u32[]{:S(2)}) copy-start(pred[512]{0:T(512)(128)(4,1)} %lt.49) | copy-start | bytes 1540
  64.1 2.8 %copy-start.1 = (f32[4,1024,128]{1,2,0:T(8,128)S(1)}, f32[4,1024,128]{1,2,0:T(8,128)}, u32[]{:S(2)}) copy-start(f32[4,1024,128]{1,2,0:T(8,128)} %get-tuple-element.41) | copy-start | bytes 6291460
  66.9 0.9 %copy-start.4 = (bf16[1,128,512]{1,2,0:T(8,128)(2,1)S(1)}, bf16[1,128,512]{1,2,0:T(8,128)(2,1)}, u32[]{:S(2)}) copy-start(bf16[1,128,512]{1,2,0:T(8,128)(2,1)} %copy.65) | copy-start | bytes 393220
where the time goes:
time: 72.9 us; the launch traced here: 72.4 us
  waiting for transfers between devices  22.8 us (31%)
  local copies, waits for them, and re-layouts  16.2 us (22%)
  starting transfers between devices  11.5 us (16%)
  other arithmetic  10 us (14%)
  matrix products  8.93 us (12%)
  between operations  2.88 us (4%)
    all_to_all x1, waiting for transfers between devices, shards(): lax.all_to_all(outgoing, 'pg', split_axis=0, concat_axis=0, tiled=True)  18 us
    all_to_all x1, starting transfers between devices, shards(): lax.all_to_all(fresh_out, 'pg', split_axis=0, concat_axis=0, tiled=True)  6.61 us
    dot_general x2, matrix products, absorb(): jnp.einsum('hqk,khd->hqd', weights.astype(jnp.bfloat16), value_rows, pref...  5.35 us
    all_to_all x1, starting transfers between devices, shards(): lax.all_to_all(outgoing, 'pg', split_axis=0, concat_axis=0, tiled=True)  4.93 us
    all_to_all x1, waiting for transfers between devices, shards(): lax.all_to_all(fresh_out, 'pg', split_axis=0, concat_axis=0, tiled=True)  4.83 us
    dot_general x2, matrix products, absorb(): jnp.einsum('hqd,khd->hqk', query_heads, key_rows, preferred_element_type=...  3.58 us
    reduce_sum x2, other arithmetic, absorb(): new_total = old_total * factor + jnp.sum(weights, axis=-1)  2.88 us
    slice x2, local copies, waits for them, and re-layouts, absorb(): key_rows = block_rows[:, :kv_width].reshape(-1, head_count, head_width)  2.3 us
  transfers between devices with their start and end apart: 2, of which 2 were waited for; matrix products, arithmetic and copies ran while one was open for 14% of the time, Pallas kernels for 0%

commit v1 on v0

v1 whole, which is shorter than its diff:
```python
import math

import jax
import jax.numpy as jnp
from jax import lax
from jax.experimental import pallas as pl
from jax.experimental.pallas import tpu as pltpu
from jax.sharding import PartitionSpec as P

Q_HEADS = 32
KV_HEADS = 4
HEAD_DIM = 128
PER_KV = Q_HEADS // KV_HEADS
KV_WIDTH = KV_HEADS * HEAD_DIM

ROPE_BASE = 1000000.0
MASKED = -1e30
SCALE = HEAD_DIM ** -0.5 / math.log(2.0)
CHUNK = 256

SMEM = pl.BlockSpec(memory_space=pltpu.SMEM)
VMEM = pl.BlockSpec(memory_space=pltpu.VMEM)
ANY = pl.BlockSpec(memory_space=pl.ANY)


def params(mib):
    return pltpu.CompilerParams(vmem_limit_bytes=mib * 1024 * 1024)


def column(head):
    return slice(head * HEAD_DIM, (head + 1) * HEAD_DIM)


def angle_tables(length, rows):
    half = HEAD_DIM // 2
    lane = lax.broadcasted_iota(jnp.int32, (1, HEAD_DIM), 1)
    step = jnp.where(lane < half, lane, lane - half).astype(jnp.float32)
    freqs = jnp.exp(step * (-math.log(ROPE_BASE) / half))
    positions = (length + lax.broadcasted_iota(jnp.int32, (rows, HEAD_DIM), 0)).astype(jnp.float32)
    angles = positions * freqs
    return jnp.cos(angles), jnp.where(lane < half, -1.0, 1.0) * jnp.sin(angles)


def turn(x, cosine, sine):
    x = x.astype(jnp.float32)
    return (x * cosine + pltpu.roll(x, HEAD_DIM // 2, 1) * sine).astype(jnp.bfloat16)


def front_kernel(
    me_ref, assign_any, length_any, owner_any, block_any, pool_ref,
    new_ref, cos_ref, sin_ref, send_ref,
    assign_ref, length_ref, owner_ref, block_ref, rows_ref, fresh_ref, small_sems, pool_sems, fresh_sems,
):
    groups, _, width = send_ref.shape
    slots = pool_ref.shape[1]
    new_count = block_any.shape[0]
    count = new_count // groups
    smalls = [
        pltpu.make_async_copy(assign_any, assign_ref, small_sems.at[0]),
        pltpu.make_async_copy(length_any, length_ref, small_sems.at[1]),
        pltpu.make_async_copy(owner_any, owner_ref, small_sems.at[2]),
        pltpu.make_async_copy(block_any, block_ref, small_sems.at[3]),
    ]
    for copy in smalls:
        copy.start()
    smalls[0].wait()

    def pool_copy(g, part):
        return pltpu.make_async_copy(
            pool_ref.at[assign_ref[g], :, pl.ds(part * width, width)],
            send_ref.at[g, pl.ds(part * slots, slots), :],
            pool_sems.at[part, g],
        )

    for g in range(groups):
        pool_copy(g, 0).start()
        pool_copy(g, 1).start()
    for copy in smalls[1:]:
        copy.wait()
    request = assign_ref[me_ref[0]]
    cosine, sine = angle_tables(length_ref[request], new_count)
    cos_ref[...] = cosine
    sin_ref[...] = sine
    for head in range(KV_HEADS):
        turned = turn(block_ref[:, column(head)], cosine, sine)
        new_ref[:, column(head)] = turned
        rows_ref[head] = turned.astype(jnp.float32)
    for head in range(KV_HEADS, 2 * KV_HEADS):
        new_ref[:, column(head)] = block_ref[:, column(head)]
        rows_ref[head] = block_ref[:, column(head)].astype(jnp.float32)

    def fresh_copy(residue):
        return pltpu.make_async_copy(
            fresh_ref.at[residue],
            send_ref.at[owner_ref[request, residue], pl.ds(2 * slots, 2 * count), :],
            fresh_sems.at[residue],
        )

    for residue in range(groups):
        for head in range(KV_HEADS):
            pair = [
                rows_ref[part * KV_HEADS + head, pl.ds(residue, count, stride=groups), :] for part in range(2)
            ]
            fresh_ref[residue, :, column(head)] = jnp.concatenate(pair, axis=0).astype(jnp.bfloat16)
        fresh_copy(residue).start()
    for g in range(groups):
        pool_copy(g, 0).wait()
        pool_copy(g, 1).wait()
        fresh_copy(g).wait()


def front(me, assignment, prefix_len, owner_map, block_kv, pool):
    groups, slots, width = pool.shape
    new_count = block_kv.shape[0]
    count = new_count // groups
    table = jax.ShapeDtypeStruct((new_count, HEAD_DIM), jnp.float32)
    return pl.pallas_call(
        front_kernel,
        out_shape=(
            jax.ShapeDtypeStruct(block_kv.shape, jnp.bfloat16),
            table,
            table,
            jax.ShapeDtypeStruct((groups, 2 * slots + 2 * count, width // 2), jnp.bfloat16),
        ),
        in_specs=[SMEM, ANY, ANY, ANY, ANY, ANY],
        out_specs=(VMEM, VMEM, VMEM, ANY),
        scratch_shapes=[
            pltpu.SMEM(assignment.shape, jnp.int32),
            pltpu.SMEM(prefix_len.shape, jnp.int32),
            pltpu.SMEM(owner_map.shape, jnp.int32),
            pltpu.VMEM(block_kv.shape, jnp.bfloat16),
            pltpu.VMEM((2 * KV_HEADS, new_count, HEAD_DIM), jnp.float32),
            pltpu.VMEM((groups, 2 * count, width // 2), jnp.bfloat16),
            pltpu.SemaphoreType.DMA((4,)),
            pltpu.SemaphoreType.DMA((2, groups)),
            pltpu.SemaphoreType.DMA((groups,)),
        ],
        compiler_params=params(60),
        name="front",
    )(me, assignment, prefix_len, owner_map, block_kv, pool)


def query_kernel(me_ref, assign_ref, length_ref, stripe_ref, q_ref, cos_ref, sin_ref, rot_ref, bias_ref):
    new_count = q_ref.shape[0]
    groups = assign_ref.shape[0]
    span = bias_ref.shape[1]
    slots = span // groups
    request = assign_ref[me_ref[0]]
    length = length_ref[request]
    lane = lax.broadcasted_iota(jnp.int32, (8, span), 1)
    holder, slot = lane // slots, lane % slots

    def visit(residue, bias):
        live = (holder == stripe_ref[request, residue]) & (slot * groups + residue < length)
        return jnp.where(live, 0.0, bias)

    bias_ref[...] = lax.fori_loop(0, groups, visit, jnp.full((8, span), MASKED, jnp.float32))
    cosine, sine = cos_ref[...], sin_ref[...]
    for head in range(Q_HEADS):
        rows = slice((head % PER_KV) * new_count, (head % PER_KV + 1) * new_count)
        rot_ref[head // PER_KV, rows, :] = turn(q_ref[:, column(head)], cosine, sine)


def rotate_queries(me, assignment, prefix_len, stripe_map, queries, cosine, sine, span):
    new_count = queries.shape[0]
    return pl.pallas_call(
        query_kernel,
        out_shape=(
            jax.ShapeDtypeStruct((KV_HEADS, PER_KV * new_count, HEAD_DIM), jnp.bfloat16),
            jax.ShapeDtypeStruct((8, span), jnp.float32),
        ),
        in_specs=[SMEM, SMEM, SMEM, SMEM, VMEM, VMEM, VMEM],
        out_specs=(VMEM, VMEM),
        compiler_params=params(32),
        name="rotate_queries",
    )(me, assignment, prefix_len, stripe_map, queries, cosine, sine)


def attend_kernel(assign_ref, rot_ref, bias_ref, new_ref, got_ref, out_ref, decode_ref, done_ref, out_sems):
    new_count = new_ref.shape[0]
    pieces, rows_in, _ = got_ref.shape
    groups = assign_ref.shape[0]
    span = bias_ref.shape[1]
    slots = span // pieces
    count = new_count // groups
    if decode_ref is not None:
        for g in range(groups):
            for part in range(2):
                decode_ref[assign_ref[g], :, part * KV_WIDTH : (part + 1) * KV_WIDTH] = got_ref[
                    g, 2 * slots : 2 * slots + 2 * count, :
                ][part * count : (part + 1) * count]
    bias = bias_ref[0:1, :]
    token = lax.broadcasted_iota(jnp.int32, (CHUNK, new_count), 0) % new_count
    causal = jnp.where(lax.broadcasted_iota(jnp.int32, (CHUNK, new_count), 1) <= token, 0.0, MASKED)
    ones = jnp.ones((span + new_count, HEAD_DIM), jnp.bfloat16)
    per_head = PER_KV * new_count // CHUNK
    keys, values = {}, {}

    def scores_of(at):
        head, chunk = divmod(at, per_head)
        if chunk == 0:
            lanes = column(head)
            parts = [got_ref[i, 0:slots, lanes] for i in range(pieces)] + [new_ref[:, lanes]]
            keys[head] = jnp.concatenate(parts, axis=0)
            parts = [got_ref[i, slots : 2 * slots, lanes] for i in range(pieces)]
            parts.append(new_ref[:, column(KV_HEADS + head)])
            values[head] = jnp.concatenate([jnp.concatenate(parts, axis=0), ones], axis=1)
        query = rot_ref[head, chunk * CHUNK : (chunk + 1) * CHUNK, :]
        return lax.dot_general(query, keys[head], (((1,), (1,)), ((), ())), preferred_element_type=jnp.float32)

    def out_copy(head):
        width = PER_KV * HEAD_DIM
        return pltpu.make_async_copy(
            done_ref.at[head], out_ref.at[:, pl.ds(head * width, width)], out_sems.at[head]
        )

    total_chunks = KV_HEADS * per_head
    ahead = scores_of(0)
    for at in range(total_chunks):
        scores = ahead
        if at + 1 < total_chunks:
            ahead = scores_of(at + 1)
        head, chunk = divmod(at, per_head)
        scores = jnp.concatenate([scores[:, :span] * SCALE + bias, scores[:, span:] * SCALE + causal], axis=1)
        weights = jnp.exp2(scores - jnp.max(scores, axis=1, keepdims=True)).astype(jnp.bfloat16)
        summed = jnp.dot(weights, values[head], preferred_element_type=jnp.float32)
        result = (summed[:, :HEAD_DIM] / summed[:, HEAD_DIM:]).astype(jnp.bfloat16)
        for row in range(CHUNK // new_count):
            done_ref[head, :, column(chunk * (CHUNK // new_count) + row)] = result[
                row * new_count : (row + 1) * new_count
            ]
        if chunk == per_head - 1:
            out_copy(head).start()
    for head in range(KV_HEADS):
        out_copy(head).wait()


def attend(assignment, rot, bias, new_kv, got, unpack):
    new_count = new_kv.shape[0]
    groups = assignment.shape[0]
    shapes = [jax.ShapeDtypeStruct((new_count, Q_HEADS * HEAD_DIM), jnp.bfloat16)]
    if unpack:
        shapes.append(jax.ShapeDtypeStruct((groups, new_count // groups, 2 * KV_WIDTH), jnp.bfloat16))

    def kernel(*refs):
        refs = list(refs)
        if not unpack:
            refs.insert(6, None)
        attend_kernel(*refs)

    return pl.pallas_call(
        kernel,
        out_shape=tuple(shapes),
        in_specs=[SMEM, VMEM, VMEM, VMEM, VMEM],
        out_specs=(ANY, VMEM)[: len(shapes)],
        scratch_shapes=[
            pltpu.VMEM((KV_HEADS, new_count, PER_KV * HEAD_DIM), jnp.bfloat16),
            pltpu.SemaphoreType.DMA((KV_HEADS,)),
        ],
        compiler_params=params(32),
        name="attend",
    )(assignment, rot, bias, new_kv, got)


def new_rows_kernel(me_ref, assign_ref, length_ref, block_ref, new_ref, cos_ref, sin_ref):
    cosine, sine = angle_tables(length_ref[assign_ref[me_ref[0]]], block_ref.shape[0])
    cos_ref[...] = cosine
    sin_ref[...] = sine
    for head in range(KV_HEADS):
        new_ref[:, column(head)] = turn(block_ref[:, column(head)], cosine, sine)
    new_ref[:, KV_WIDTH:] = block_ref[:, KV_WIDTH:]


def inverse(table):
    places = jnp.arange(table.shape[0], dtype=jnp.int32)
    return jnp.sum(jnp.where(table[None, :] == places[:, None], places, 0), axis=1)


def small_pieces(me, assignment, prefix_len, stripe_map, owner_map, queries, block_kv, pool):
    groups, slots, width = pool.shape
    new_count = block_kv.shape[0]
    count = new_count // groups
    table = jax.ShapeDtypeStruct((new_count, HEAD_DIM), jnp.float32)
    new_kv, cosine, sine = pl.pallas_call(
        new_rows_kernel,
        out_shape=(jax.ShapeDtypeStruct(block_kv.shape, jnp.bfloat16), table, table),
        in_specs=[SMEM, SMEM, SMEM, VMEM],
        out_specs=(VMEM, VMEM, VMEM),
        compiler_params=params(32),
        name="new_rows",
    )(me, assignment, prefix_len, block_kv)
    spread = jnp.transpose(new_kv.reshape(count, groups, width), (1, 0, 2))
    fresh = spread[inverse(owner_map[assignment[me[0]]])]
    send = jnp.concatenate([pool[assignment], fresh], axis=1)
    got = lax.all_to_all(send, "pg", split_axis=0, concat_axis=0, tiled=True)
    rot, bias = rotate_queries(
        me, assignment, prefix_len, stripe_map, queries, cosine, sine, groups * slots
    )
    keys = got[:, :slots].reshape(groups * slots, width)
    keys = jnp.concatenate([keys[:, :KV_WIDTH], keys[:, KV_WIDTH:]], axis=0)[None]
    (attended,) = attend(assignment, rot, bias, new_kv, keys, False)
    return attended, got[inverse(assignment), slots:]


def shards(queries, block_kv, pool_kv, prefix_len, assignment, stripe_map, owner_map):
    queries, block_kv, pool = queries[0], block_kv[0], pool_kv[0]
    groups, slots, _ = pool.shape
    me = lax.axis_index("pg").astype(jnp.int32).reshape(1)
    if slots % 16 or (2 * queries.shape[0] // groups) % 16:
        attended, decode_kv = small_pieces(
            me, assignment, prefix_len, stripe_map, owner_map, queries, block_kv, pool
        )
        return (attended[None], decode_kv[None])
    new_kv, cosine, sine, send = front(me, assignment, prefix_len, owner_map, block_kv, pool)
    got = lax.all_to_all(send, "pg", split_axis=0, concat_axis=0, tiled=True)
    rot, bias = rotate_queries(
        me, assignment, prefix_len, stripe_map, queries, cosine, sine, groups * slots
    )
    attended, decode_kv = attend(assignment, rot, bias, new_kv, got, True)
    return (attended[None], decode_kv[None])


def solution(mesh):
    return jax.shard_map(
        shards,
        mesh=mesh,
        in_specs=(
            P(("rep", "pg"), None, None),
            P(("rep", "pg"), None, None),
            P(("rep", "pg"), None, None, None),
            P("rep"),
            P("rep"),
            P("rep", None),
            P("rep", None),
        ),
        out_specs=(P(("rep", "pg"), None, None), P(("rep", "pg"), None, None, None)),
        check_vma=False,
    )
```

time: 72.9 us -> 80.5 us (1.10)
  the two profiles are of different devices: /device:TPU:11 before, /device:TPU:15 now
where the time goes in v1:
time: 80.5 us; the launch traced here: 80.2 us
  Pallas kernels  41.9 us (52%)
  waiting for transfers between devices  27.2 us (34%)
  starting transfers between devices  6.7 us (8%)
  local copies, waits for them, and re-layouts  3.62 us (4%)
    pallas_call x1, Pallas kernels, front(): pl.pallas_call(front_kernel, out_shape=(jax.ShapeDtypeStruct(block_kv.sha...  34.7 us
    all_to_all x1, waiting for transfers between devices, shards(): got = lax.all_to_all(send, 'pg', split_axis=0, concat_axis=0, tiled=True)  27.2 us
    all_to_all x1, starting transfers between devices, shards(): got = lax.all_to_all(send, 'pg', split_axis=0, concat_axis=0, tiled=True)  6.7 us
    pallas_call x1, Pallas kernels, attend(): pl.pallas_call(kernel, out_shape=tuple(shapes), in_specs=[SMEM, VMEM, VME...  5.92 us
    unnamed x16, local copies, waits for them, and re-layouts  3.62 us
  transfers between devices with their start and end apart: 1, of which 1 were waited for; matrix products, arithmetic and copies ran while one was open for 0% of the time, Pallas kernels for 2%

profile of v1, /device:TPU:15, one launch (start us, length us, event | category | flops | bytes accessed | tf_op | source)
XLA Modules:
  0.0 80.2 jit_solution(5364596838718997852)
XLA Ops:
  0.6 34.7 %front.1 = (bf16[128,1024]{1,0:T(8,128)(2,1)}, f32[128,128]{1,0:T(8,128)}, f32[128,128]{1,0:T(8,128)}, bf16[16,80,512]{2,1,0:T(8,128)(2,1)}) custom-call(s32[1]{0:T(128)} %bitcast.me_ref, s32[16]{0:T(128)} %refs_0_.1, s32[16]{0:T(128)} %length_ref.1, s32[16,16]{1,0:T(8,128)} %owner_any.1, bf16[128,1024]{1,0:T(8,128)(2,1)} %bitcast.8, ...), custom_call_target="tpu_custom_call" | custom-call | tf_op jit(solution)/shard_map/front/pallas_call | solution.py:117
  35.4 0.0 copy-start
  35.4 0.0 copy-start.2
  35.4 0.0 copy-start.3
  35.4 6.7 %all-to-all-start = ((bf16[16,80,512]{2,1,0:T(8,128)(2,1)}), bf16[16,80,512]{2,1,0:T(8,128)(2,1)S(1)}, u32[]{:S(2)}, u32[]{:S(2)}) async-start(bf16[16,80,512]{2,1,0:T(8,128)(2,1)} %get-tuple-element.15), calls=%async_computation | async-start | bytes 2621440 | tf_op jit(solution)/shard_map/all_to_all | solution.py:315
  42.1 0.0 copy-done
  42.1 0.0 copy-done.2
  42.1 0.0 copy-done.3
  42.1 0.0 copy-start.4
  42.1 0.7 copy-done.4
  42.8 0.0 copy-start.5
  42.8 0.7 copy-done.5
  43.5 0.0 copy-start.7
  43.5 0.7 copy-done.7
  44.1 1.3 %rotate_queries.1 = (bf16[4,1024,128]{2,1,0:T(8,128)(2,1)S(1)}, f32[8,512]{1,0:T(8,128)S(1)}) custom-call(s32[1]{0:T(128)} %bitcast.me_ref, s32[16]{0:T(128)S(1)} %copy-done.5, s32[16]{0:T(128)S(1)} %copy-done.7, s32[16,16]{1,0:T(8,128)S(1)} %copy-done.4, bf16[128,4096]{1,0:T(8,128)(2,1)S(1)} %bitcast.6, f32[128,128]{1,0:T(8,128)S(1)} %copy-done.2, ...), custom_call_target="tpu_custom_call" | custom-call | tf_op jit(solution)/shard_map/rotate_queries/pallas_call | solution.py:166
  45.4 27.2 %all-to-all-done.refs_4_ = bf16[16,80,512]{2,1,0:T(8,128)(2,1)S(1)} async-done(((bf16[16,80,512]{2,1,0:T(8,128)(2,1)}), bf16[16,80,512]{2,1,0:T(8,128)(2,1)S(1)}, u32[]{:S(2)}, u32[]{:S(2)}) %all-to-all-start) | async-done | bytes 1310752 | tf_op jit(solution)/shard_map/all_to_all | solution.py:315
  72.7 0.0 copy-start.1
  72.7 0.9 %copy-done.1 = bf16[128,1024]{1,0:T(8,128)(2,1)S(1)} copy-done((bf16[128,1024]{1,0:T(8,128)(2,1)S(1)}, bf16[128,1024]{1,0:T(8,128)(2,1)}, u32[]{:S(2)}) %copy-start.1) | copy-done | bytes 262168
  73.6 0.0 copy-start.6
  73.6 0.7 copy-done.6
  74.3 5.9 %attend.1 = (bf16[128,4096]{1,0:T(8,128)(2,1)}, bf16[16,8,1024]{2,1,0:T(8,128)(2,1)}) custom-call(s32[16]{0:T(128)S(1)} %copy-done.6, bf16[4,1024,128]{2,1,0:T(8,128)(2,1)S(1)} %get-tuple-element.12.refs_1_, f32[8,512]{1,0:T(8,128)S(1)} %get-tuple-element.13.refs_2_, bf16[128,1024]{1,0:T(8,128)(2,1)S(1)} %copy-done.1, ...), custom_call_target="tpu_custom_call" | custom-call | tf_op jit(solution)/shard_map/attend/pallas_call | solution.py:251
Async XLA Ops:
  35.4 6.7 %copy-start = (bf16[1,128,4096]{2,1,0:T(8,128)(2,1)S(1)}, bf16[1,128,4096]{2,1,0:T(8,128)(2,1)}, u32[]{:S(2)}) copy-start(bf16[1,128,4096]{2,1,0:T(8,128)(2,1)} %param.7) | copy-start | bytes 3145732
  35.4 6.7 %copy-start.2 = (f32[128,128]{1,0:T(8,128)S(1)}, f32[128,128]{1,0:T(8,128)}, u32[]{:S(2)}) copy-start(f32[128,128]{1,0:T(8,128)} %get-tuple-element.10.cos_ref) | copy-start | bytes 196612
  35.4 6.7 %copy-start.3 = (f32[128,128]{1,0:T(8,128)S(1)}, f32[128,128]{1,0:T(8,128)}, u32[]{:S(2)}) copy-start(f32[128,128]{1,0:T(8,128)} %get-tuple-element.11.sin_ref) | copy-start | bytes 196612
  35.4 37.3 %all-to-all-start = ((bf16[16,80,512]{2,1,0:T(8,128)(2,1)}), bf16[16,80,512]{2,1,0:T(8,128)(2,1)S(1)}, u32[]{:S(2)}, u32[]{:S(2)}) async-start(bf16[16,80,512]{2,1,0:T(8,128)(2,1)} %get-tuple-element.15), calls=%async_computation | async-start | bytes 2621440 | tf_op jit(solution)/shard_map/all_to_all | solution.py:315
  42.1 0.7 copy-start.4
  42.8 0.7 copy-start.5
  43.5 0.7 copy-start.7
  72.7 1.0 %copy-start.1 = (bf16[128,1024]{1,0:T(8,128)(2,1)S(1)}, bf16[128,1024]{1,0:T(8,128)(2,1)}, u32[]{:S(2)}) copy-start(bf16[128,1024]{1,0:T(8,128)(2,1)} %get-tuple-element.14.refs_3_) | copy-start | bytes 786436
  73.6 0.7 copy-start.6

commit v2 on v1

v2 whole, which is shorter than its diff:
```python
import functools
import math

import jax
import jax.numpy as jnp
from jax import lax
from jax.experimental import pallas as pl
from jax.experimental.pallas import tpu as pltpu
from jax.sharding import PartitionSpec as P

Q_HEADS = 32
KV_HEADS = 4
HEAD_DIM = 128
PER_KV = Q_HEADS // KV_HEADS
KV_WIDTH = KV_HEADS * HEAD_DIM

ROPE_BASE = 1000000.0
MASKED = -1e30
SCALE = HEAD_DIM ** -0.5 / math.log(2.0)
CHUNK = 256

SMEM = pl.BlockSpec(memory_space=pltpu.SMEM)
VMEM = pl.BlockSpec(memory_space=pltpu.VMEM)
ANY = pl.BlockSpec(memory_space=pl.ANY)


def params(mib):
    return pltpu.CompilerParams(vmem_limit_bytes=mib * 1024 * 1024)


def column(head):
    return slice(head * HEAD_DIM, (head + 1) * HEAD_DIM)


def angle_tables(length, rows):
    half = HEAD_DIM // 2
    lane = lax.broadcasted_iota(jnp.int32, (1, HEAD_DIM), 1)
    step = jnp.where(lane < half, lane, lane - half).astype(jnp.float32)
    freqs = jnp.exp(step * (-math.log(ROPE_BASE) / half))
    positions = (length + lax.broadcasted_iota(jnp.int32, (rows, HEAD_DIM), 0)).astype(jnp.float32)
    angles = positions * freqs
    return jnp.cos(angles), jnp.where(lane < half, -1.0, 1.0) * jnp.sin(angles)


def turn(x, cosine, sine):
    x = x.astype(jnp.float32)
    return (x * cosine + pltpu.roll(x, HEAD_DIM // 2, 1) * sine).astype(jnp.bfloat16)


def front_kernel(
    me_ref, assign_any, length_any, owner_any, block_any, pool_any, *refs
):
    groups, slots, _ = pool_any.shape
    send_refs, refs = refs[:groups], refs[groups:]
    assign_ref, length_ref, owner_ref, residue_ref, block_ref, rows_ref, small_sems, pool_sems = refs
    width = send_refs[0].shape[1]
    new_count = block_any.shape[0]
    count = new_count // groups
    smalls = [
        pltpu.make_async_copy(assign_any, assign_ref, small_sems.at[0]),
        pltpu.make_async_copy(length_any, length_ref, small_sems.at[1]),
        pltpu.make_async_copy(owner_any, owner_ref, small_sems.at[2]),
        pltpu.make_async_copy(block_any, block_ref, small_sems.at[3]),
    ]
    for copy in smalls:
        copy.start()
    me = me_ref[0]
    smalls[0].wait()

    def pool_copy(t, part):
        return pltpu.make_async_copy(
            pool_any.at[assign_ref[me ^ t], :, pl.ds(part * width, width)],
            send_refs[t].at[pl.ds(part * slots, slots), :],
            pool_sems.at[part, t],
        )

    for t in range(groups):
        pool_copy(t, 0).start()
        pool_copy(t, 1).start()
    for copy in smalls[1:]:
        copy.wait()
    request = assign_ref[me]
    for residue in range(groups):
        residue_ref[owner_ref[request, residue]] = residue
    cosine, sine = angle_tables(length_ref[request], new_count)
    for head in range(KV_HEADS):
        turned = turn(block_ref[:, column(head)], cosine, sine)
        rows_ref[head] = turned.astype(jnp.float32)
        rows_ref[KV_HEADS + head] = block_ref[:, column(KV_HEADS + head)].astype(jnp.float32)
    for t in range(groups):
        residue = residue_ref[me ^ t]
        for head in range(KV_HEADS):
            pair = [
                rows_ref[part * KV_HEADS + head, pl.ds(residue, count, stride=groups), :] for part in range(2)
            ]
            send_refs[t][2 * slots : 2 * slots + 2 * count, column(head)] = jnp.concatenate(
                pair, axis=0
            ).astype(jnp.bfloat16)
    for t in range(groups):
        pool_copy(t, 0).wait()
        pool_copy(t, 1).wait()


def front(me, assignment, prefix_len, owner_map, block_kv, pool):
    groups, slots, width = pool.shape
    new_count = block_kv.shape[0]
    count = new_count // groups
    return pl.pallas_call(
        front_kernel,
        out_shape=[jax.ShapeDtypeStruct((2 * slots + 2 * count, width // 2), jnp.bfloat16)] * groups,
        in_specs=[SMEM, ANY, ANY, ANY, ANY, ANY],
        out_specs=[VMEM] * groups,
        scratch_shapes=[
            pltpu.SMEM(assignment.shape, jnp.int32),
            pltpu.SMEM(prefix_len.shape, jnp.int32),
            pltpu.SMEM(owner_map.shape, jnp.int32),
            pltpu.SMEM(assignment.shape, jnp.int32),
            pltpu.VMEM(block_kv.shape, jnp.bfloat16),
            pltpu.VMEM((2 * KV_HEADS, new_count, HEAD_DIM), jnp.float32),
            pltpu.SemaphoreType.DMA((4,)),
            pltpu.SemaphoreType.DMA((2, groups)),
        ],
        compiler_params=params(60),
        name="front",
    )(me, assignment, prefix_len, owner_map, block_kv, pool)


def query_kernel(me_ref, assign_ref, length_ref, stripe_ref, q_ref, block_ref, rot_ref, bias_ref, new_ref, order_ref):
    new_count = q_ref.shape[0]
    groups = assign_ref.shape[0]
    span = bias_ref.shape[1]
    slots = span // groups
    me = me_ref[0]
    request = assign_ref[me]
    length = length_ref[request]
    lane = lax.broadcasted_iota(jnp.int32, (8, span), 1)
    holder, slot = (lane // slots) ^ me, lane % slots

    def visit(residue, bias):
        live = (holder == stripe_ref[request, residue]) & (slot * groups + residue < length)
        return jnp.where(live, 0.0, bias)

    bias_ref[...] = lax.fori_loop(0, groups, visit, jnp.full((8, span), MASKED, jnp.float32))
    place = lax.broadcasted_iota(jnp.int32, order_ref.shape, 1)

    def name(t, order):
        return jnp.where(place == t, assign_ref[me ^ t], order)

    order_ref[...] = lax.fori_loop(0, groups, name, jnp.zeros(order_ref.shape, jnp.int32))
    cosine, sine = angle_tables(length, new_count)
    for head in range(KV_HEADS):
        new_ref[:, column(head)] = turn(block_ref[:, column(head)], cosine, sine)
    new_ref[:, KV_WIDTH:] = block_ref[:, KV_WIDTH:]
    for head in range(Q_HEADS):
        rows = slice((head % PER_KV) * new_count, (head % PER_KV + 1) * new_count)
        rot_ref[head // PER_KV, rows, :] = turn(q_ref[:, column(head)], cosine, sine)


def rotate_queries(me, assignment, prefix_len, stripe_map, queries, block_kv, span):
    new_count = queries.shape[0]
    return pl.pallas_call(
        query_kernel,
        out_shape=(
            jax.ShapeDtypeStruct((KV_HEADS, PER_KV * new_count, HEAD_DIM), jnp.bfloat16),
            jax.ShapeDtypeStruct((8, span), jnp.float32),
            jax.ShapeDtypeStruct(block_kv.shape, jnp.bfloat16),
            jax.ShapeDtypeStruct((8, HEAD_DIM), jnp.int32),
        ),
        in_specs=[SMEM, SMEM, SMEM, SMEM, VMEM, VMEM],
        out_specs=(VMEM, VMEM, VMEM, VMEM),
        compiler_params=params(32),
        name="rotate_queries",
    )(me, assignment, prefix_len, stripe_map, queries, block_kv)


def attend_kernel(unpack, pieces, order_vmem, rot_ref, bias_ref, new_ref, *refs):
    got_refs, refs = refs[:pieces], refs[pieces:]
    out_ref, refs = refs[0], refs[1:]
    if unpack:
        decode_ref, refs = refs[0], refs[1:]
    done_ref, order_ref, out_sems, order_sem = refs
    new_count = new_ref.shape[0]
    span = bias_ref.shape[1]
    slots = span // pieces
    order_copy = pltpu.make_async_copy(order_vmem, order_ref, order_sem)
    order_copy.start()
    bias = bias_ref[0:1, :]
    token = lax.broadcasted_iota(jnp.int32, (CHUNK, new_count), 0) % new_count
    causal = jnp.where(lax.broadcasted_iota(jnp.int32, (CHUNK, new_count), 1) <= token, 0.0, MASKED)
    ones = jnp.ones((span + new_count, HEAD_DIM), jnp.bfloat16)
    per_head = PER_KV * new_count // CHUNK
    keys, values = {}, {}

    def scores_of(at):
        head, chunk = divmod(at, per_head)
        if chunk == 0:
            lanes = column(head)
            parts = [got[0:slots, lanes] for got in got_refs] + [new_ref[:, lanes]]
            keys[head] = jnp.concatenate(parts, axis=0)
            parts = [got[slots : 2 * slots, lanes] for got in got_refs]
            parts.append(new_ref[:, column(KV_HEADS + head)])
            values[head] = jnp.concatenate([jnp.concatenate(parts, axis=0), ones], axis=1)
        query = rot_ref[head, chunk * CHUNK : (chunk + 1) * CHUNK, :]
        return lax.dot_general(query, keys[head], (((1,), (1,)), ((), ())), preferred_element_type=jnp.float32)

    def out_copy(head):
        width = PER_KV * HEAD_DIM
        return pltpu.make_async_copy(
            done_ref.at[head], out_ref.at[:, pl.ds(head * width, width)], out_sems.at[head]
        )

    total_chunks = KV_HEADS * per_head
    ahead = scores_of(0)
    for at in range(total_chunks):
        scores = ahead
        if at + 1 < total_chunks:
            ahead = scores_of(at + 1)
        head, chunk = divmod(at, per_head)
        scores = jnp.concatenate([scores[:, :span] * SCALE + bias, scores[:, span:] * SCALE + causal], axis=1)
        weights = jnp.exp2(scores - jnp.max(scores, axis=1, keepdims=True)).astype(jnp.bfloat16)
        summed = jnp.dot(weights, values[head], preferred_element_type=jnp.float32)
        result = (summed[:, :HEAD_DIM] / summed[:, HEAD_DIM:]).astype(jnp.bfloat16)
        for row in range(CHUNK // new_count):
            done_ref[head, :, column(chunk * (CHUNK // new_count) + row)] = result[
                row * new_count : (row + 1) * new_count
            ]
        if chunk == per_head - 1:
            out_copy(head).start()
    order_copy.wait()
    if unpack:
        count = decode_ref.shape[1]
        for t, got in enumerate(got_refs):
            rows = got[2 * slots : 2 * slots + 2 * count, :]
            for part in range(2):
                decode_ref[order_ref[0, t], :, part * KV_WIDTH : (part + 1) * KV_WIDTH] = rows[
                    part * count : (part + 1) * count
                ]
    for head in range(KV_HEADS):
        out_copy(head).wait()


def attend(order, rot, bias, new_kv, got, count):
    new_count = new_kv.shape[0]
    shapes = [jax.ShapeDtypeStruct((new_count, Q_HEADS * HEAD_DIM), jnp.bfloat16)]
    if count:
        shapes.append(jax.ShapeDtypeStruct((new_count // count, count, 2 * KV_WIDTH), jnp.bfloat16))
    return pl.pallas_call(
        functools.partial(attend_kernel, count > 0, len(got)),
        out_shape=tuple(shapes),
        in_specs=[VMEM] * (4 + len(got)),
        out_specs=(ANY, VMEM)[: len(shapes)],
        scratch_shapes=[
            pltpu.VMEM((KV_HEADS, new_count, PER_KV * HEAD_DIM), jnp.bfloat16),
            pltpu.SMEM(order.shape, jnp.int32),
            pltpu.SemaphoreType.DMA((KV_HEADS,)),
            pltpu.SemaphoreType.DMA,
        ],
        compiler_params=params(32),
        name="attend",
    )(order, rot, bias, new_kv, *got)


def inverse(table):
    places = jnp.arange(table.shape[0], dtype=jnp.int32)
    return jnp.sum(jnp.where(table[None, :] == places[:, None], places, 0), axis=1)


def small_pieces(me, assignment, prefix_len, stripe_map, owner_map, queries, block_kv, pool):
    groups, slots, width = pool.shape
    count = block_kv.shape[0] // groups
    rot, bias, new_kv, order = rotate_queries(
        me, assignment, prefix_len, stripe_map, queries, block_kv, groups * slots
    )
    spread = jnp.transpose(new_kv.reshape(count, groups, width), (1, 0, 2))
    fresh = spread[inverse(owner_map[assignment[me[0]]])]
    send = jnp.concatenate([pool[assignment], fresh], axis=1)
    got = lax.all_to_all(send, "pg", split_axis=0, concat_axis=0, tiled=True)
    places = jnp.arange(groups, dtype=jnp.int32) ^ me[0]
    keys = got[places, :slots].reshape(groups * slots, width)
    keys = jnp.concatenate([keys[:, :KV_WIDTH], keys[:, KV_WIDTH:]], axis=0)
    (attended,) = attend(order, rot, bias, new_kv, [keys], 0)
    return attended, got[inverse(assignment), slots:]


def exchange(blocks):
    got = [blocks[0]]
    for t in range(len(blocks) - 1, 0, -1):
        pairs = [(source, source ^ t) for source in range(len(blocks))]
        got.insert(1, lax.ppermute(blocks[t], "pg", pairs))
    return got


def shards(queries, block_kv, pool_kv, prefix_len, assignment, stripe_map, owner_map):
    queries, block_kv, pool = queries[0], block_kv[0], pool_kv[0]
    groups, slots, _ = pool.shape
    count = queries.shape[0] // groups
    me = lax.axis_index("pg").astype(jnp.int32).reshape(1)
    if slots % 16 or (2 * count) % 16 or groups > 16:
        attended, decode_kv = small_pieces(
            me, assignment, prefix_len, stripe_map, owner_map, queries, block_kv, pool
        )
        return (attended[None], decode_kv[None])
    got = exchange(front(me, assignment, prefix_len, owner_map, block_kv, pool))
    rot, bias, new_kv, order = rotate_queries(
        me, assignment, prefix_len, stripe_map, queries, block_kv, groups * slots
    )
    attended, decode_kv = attend(order, rot, bias, new_kv, got, count)
    return (attended[None], decode_kv[None])


def solution(mesh):
    return jax.shard_map(
        shards,
        mesh=mesh,
        in_specs=(
            P(("rep", "pg"), None, None),
            P(("rep", "pg"), None, None),
            P(("rep", "pg"), None, None, None),
            P("rep"),
            P("rep"),
            P("rep", None),
            P("rep", None),
        ),
        out_specs=(P(("rep", "pg"), None, None), P(("rep", "pg"), None, None, None)),
        check_vma=False,
    )
```

time: 80.5 us -> 49.7 us (0.62)
  the two profiles are of different devices: /device:TPU:15 before, /device:TPU:19 now
where the time goes in v2:
time: 49.7 us; the launch traced here: 49.5 us
  starting transfers between devices  25.4 us (51%)
  waiting for transfers between devices  12.7 us (26%)
  Pallas kernels  10.7 us (22%)
  between operations  0.71 us (1%)
    ppermute x15, starting transfers between devices, exchange(): got.insert(1, lax.ppermute(blocks[t], 'pg', pairs))  25.4 us
    ppermute x15, waiting for transfers between devices, exchange(): got.insert(1, lax.ppermute(blocks[t], 'pg', pairs))  12.7 us
    pallas_call x1, Pallas kernels, attend(): pl.pallas_call(functools.partial(attend_kernel, count > 0, len(got)), out...  5.64 us
    pallas_call x1, Pallas kernels, front(): pl.pallas_call(front_kernel, out_shape=[jax.ShapeDtypeStruct((2 * slots +...  3.32 us
    pallas_call x1, Pallas kernels, rotate_queries(): pl.pallas_call(query_kernel, out_shape=(jax.ShapeDtypeStruct((KV_HEADS, P...  1.69 us
  transfers between devices with their start and end apart: 15, of which 5 were waited for; matrix products, arithmetic and copies ran while one was open for 0% of the time, Pallas kernels for 3%

profile of v2, /device:TPU:19, one launch (start us, length us, event | category | flops | bytes accessed | tf_op | source)
XLA Modules:
  0.0 49.5 jit_solution(16832331248335416376)
XLA Ops:
  0.7 3.3 %front.1 = (bf16[80,512]{1,0:T(8,128)(2,1)}, bf16[80,512]{1,0:T(8,128)(2,1)}, bf16[80,512]{1,0:T(8,128)(2,1)}, bf16[80,512]{1,0:T(8,128)(2,1)}, bf16[80,512]{1,0...) custom-call(s32[1]{0:T(128)} %bitcast.me_ref, ...), custom_call_target="tpu_custom_call" | custom-call | tf_op jit(solution)/shard_map/front/pallas_call | solution.py:108
  4.0 0.7 %collective-permute-start = (bf16[80,512]{1,0:T(8,128)(2,1)}, bf16[80,512]{1,0:T(8,128)(2,1)S(1)}, u32[]{:S(2)}, u32[]{:S(2)}) collective-permute-start(bf16[80,512]{1,0:T(8,128)(2,1)} %get-tuple-element.29), channel_id=1, source_target_pairs={{0,1},{1,0},{2,3},{3,2},{4,5},{5,4},{6,7},{7,6},{8,9},{9,8},{10,11... | collective-permute-start | bytes 245768 | tf_op jit(solution)/shard_map/ppermute | solution.py:289
  4.7 1.3 %collective-permute-start.1 = (bf16[80,512]{1,0:T(8,128)(2,1)}, bf16[80,512]{1,0:T(8,128)(2,1)S(1)}, u32[]{:S(2)}, u32[]{:S(2)}) collective-permute-start(bf16[80,512]{1,0:T(8,128)(2,1)} %get-tuple-element.30), channel_id=1, source_target_pairs={{0,2},{1,3},{2,0},{3,1},{4,6},{5,7},{6,4},{7,5},{8,10},{9,11},{10,... | collective-permute-start | bytes 245768 | tf_op jit(solution)/shard_map/ppermute | solution.py:289
  6.0 0.5 collective-permute-start.2
  6.4 1.3 %collective-permute-start.3 = (bf16[80,512]{1,0:T(8,128)(2,1)}, bf16[80,512]{1,0:T(8,128)(2,1)S(1)}, u32[]{:S(2)}, u32[]{:S(2)}) collective-permute-start(bf16[80,512]{1,0:T(8,128)(2,1)} %get-tuple-element.32), channel_id=1, source_target_pairs={{0,4},{1,5},{2,6},{3,7},{4,0},{5,1},{6,2},{7,3},{8,12},{9,13},{10,... | collective-permute-start | bytes 245768 | tf_op jit(solution)/shard_map/ppermute | solution.py:289
  7.7 0.5 %collective-permute-start.4 = (bf16[80,512]{1,0:T(8,128)(2,1)}, bf16[80,512]{1,0:T(8,128)(2,1)S(1)}, u32[]{:S(2)}, u32[]{:S(2)}) collective-permute-start(bf16[80,512]{1,0:T(8,128)(2,1)} %get-tuple-element.33), channel_id=1, source_target_pairs={{0,5},{1,4},{2,7},{3,6},{4,1},{5,0},{6,3},{7,2},{8,13},{9,12},{10,... | collective-permute-start | bytes 245768 | tf_op jit(solution)/shard_map/ppermute | solution.py:289
  8.2 2.3 %collective-permute-start.5 = (bf16[80,512]{1,0:T(8,128)(2,1)}, bf16[80,512]{1,0:T(8,128)(2,1)S(1)}, u32[]{:S(2)}, u32[]{:S(2)}) collective-permute-start(bf16[80,512]{1,0:T(8,128)(2,1)} %get-tuple-element.34), channel_id=1, source_target_pairs={{0,6},{1,7},{2,4},{3,5},{4,2},{5,3},{6,0},{7,1},{8,14},{9,15},{10,... | collective-permute-start | bytes 245768 | tf_op jit(solution)/shard_map/ppermute | solution.py:289
  10.5 1.9 %collective-permute-start.6 = (bf16[80,512]{1,0:T(8,128)(2,1)}, bf16[80,512]{1,0:T(8,128)(2,1)S(1)}, u32[]{:S(2)}, u32[]{:S(2)}) collective-permute-start(bf16[80,512]{1,0:T(8,128)(2,1)} %get-tuple-element.35), channel_id=1, source_target_pairs={{0,7},{1,6},{2,5},{3,4},{4,3},{5,2},{6,1},{7,0},{8,15},{9,14},{10,... | collective-permute-start | bytes 245768 | tf_op jit(solution)/shard_map/ppermute | solution.py:289
  12.4 0.1 collective-permute-start.7
  12.5 1.7 %collective-permute-start.8 = (bf16[80,512]{1,0:T(8,128)(2,1)}, bf16[80,512]{1,0:T(8,128)(2,1)S(1)}, u32[]{:S(2)}, u32[]{:S(2)}) collective-permute-start(bf16[80,512]{1,0:T(8,128)(2,1)} %get-tuple-element.37), channel_id=1, source_target_pairs={{0,9},{1,8},{2,11},{3,10},{4,13},{5,12},{6,15},{7,14},{8,1},{9,0},... | collective-permute-start | bytes 245768 | tf_op jit(solution)/shard_map/ppermute | solution.py:289
  14.1 0.7 %collective-permute-start.9 = (bf16[80,512]{1,0:T(8,128)(2,1)}, bf16[80,512]{1,0:T(8,128)(2,1)S(1)}, u32[]{:S(2)}, u32[]{:S(2)}) collective-permute-start(bf16[80,512]{1,0:T(8,128)(2,1)} %get-tuple-element.38), channel_id=1, source_target_pairs={{0,10},{1,11},{2,8},{3,9},{4,14},{5,15},{6,12},{7,13},{8,2},{9,3},... | collective-permute-start | bytes 245768 | tf_op jit(solution)/shard_map/ppermute | solution.py:289
  14.8 0.6 %collective-permute-done.5.refs_6_ = bf16[80,512]{1,0:T(8,128)(2,1)S(1)} collective-permute-done((bf16[80,512]{1,0:T(8,128)(2,1)}, bf16[80,512]{1,0:T(8,128)(2,1)S(1)}, u32[]{:S(2)}, u32[]{:S(2)}) %collective-permute-start.5) | collective-permute-done | bytes 81952 | tf_op jit(solution)/shard_map/ppermute | solution.py:289
  15.4 3.2 %collective-permute-start.10 = (bf16[80,512]{1,0:T(8,128)(2,1)}, bf16[80,512]{1,0:T(8,128)(2,1)S(1)}, u32[]{:S(2)}, u32[]{:S(2)}) collective-permute-start(bf16[80,512]{1,0:T(8,128)(2,1)} %get-tuple-element.39), channel_id=1, source_target_pairs={{0,11},{1,10},{2,9},{3,8},{4,15},{5,14},{6,13},{7,12},{8,3},{9,2},... | collective-permute-start | bytes 245768 | tf_op jit(solution)/shard_map/ppermute | solution.py:289
  18.6 0.3 collective-permute-start.11
  18.9 6.9 %collective-permute-start.12 = (bf16[80,512]{1,0:T(8,128)(2,1)}, bf16[80,512]{1,0:T(8,128)(2,1)S(1)}, u32[]{:S(2)}, u32[]{:S(2)}) collective-permute-start(bf16[80,512]{1,0:T(8,128)(2,1)} %get-tuple-element.41), channel_id=1, source_target_pairs={{0,13},{1,12},{2,15},{3,14},{4,9},{5,8},{6,11},{7,10},{8,5},{9,4},... | collective-permute-start | bytes 245768 | tf_op jit(solution)/shard_map/ppermute | solution.py:289
  25.8 1.6 %collective-permute-start.13 = (bf16[80,512]{1,0:T(8,128)(2,1)}, bf16[80,512]{1,0:T(8,128)(2,1)S(1)}, u32[]{:S(2)}, u32[]{:S(2)}) collective-permute-start(bf16[80,512]{1,0:T(8,128)(2,1)} %get-tuple-element.42), channel_id=1, source_target_pairs={{0,14},{1,15},{2,12},{3,13},{4,10},{5,11},{6,8},{7,9},{8,6},{9,7},... | collective-permute-start | bytes 245768 | tf_op jit(solution)/shard_map/ppermute | solution.py:289
  27.4 2.7 %collective-permute-start.14 = (bf16[80,512]{1,0:T(8,128)(2,1)}, bf16[80,512]{1,0:T(8,128)(2,1)S(1)}, u32[]{:S(2)}, u32[]{:S(2)}) collective-permute-start(bf16[80,512]{1,0:T(8,128)(2,1)} %get-tuple-element.43), channel_id=1, source_target_pairs={{0,15},{1,14},{2,13},{3,12},{4,11},{5,10},{6,9},{7,8},{8,7},{9,6},... | collective-permute-start | bytes 245768 | tf_op jit(solution)/shard_map/ppermute | solution.py:289
  30.1 0.0 copy-start.2
  30.1 1.7 %rotate_queries.1 = (bf16[4,1024,128]{2,1,0:T(8,128)(2,1)S(1)}, f32[8,512]{1,0:T(8,128)S(1)}, bf16[128,1024]{1,0:T(8,128)(2,1)S(1)}, s32[8,128]{1,0:T(8,128)S(1)}) custom-call(s32[1]{0:T(128)} %bitcast.me_ref, s32[16]{0:T(128)S(1)} %copy-done.4, s32[16]{0:T(128)S(1)} %copy-done.5, s32[16,16]{1,0:T(8,128)S(1)} %copy-done.3, bf16[128,4096]{1,0:T(8,128)(2,1)S(1)} %bitcast.6, ...), custom_call_target="tpu_custom_call" | custom-call | tf_op jit(solution)/shard_map/rotate_queries/pallas_call | solution.py:161
  31.8 5.9 %collective-permute-done.11.refs_12_ = bf16[80,512]{1,0:T(8,128)(2,1)S(1)} collective-permute-done((bf16[80,512]{1,0:T(8,128)(2,1)}, bf16[80,512]{1,0:T(8,128)(2,1)S(1)}, u32[]{:S(2)}, u32[]{:S(2)}) %collective-permute-start.11) | collective-permute-done | bytes 81952 | tf_op jit(solution)/shard_map/ppermute | solution.py:289
  37.7 2.2 %collective-permute-done.12.refs_13_ = bf16[80,512]{1,0:T(8,128)(2,1)S(1)} collective-permute-done((bf16[80,512]{1,0:T(8,128)(2,1)}, bf16[80,512]{1,0:T(8,128)(2,1)S(1)}, u32[]{:S(2)}, u32[]{:S(2)}) %collective-permute-start.12) | collective-permute-done | bytes 81952 | tf_op jit(solution)/shard_map/ppermute | solution.py:289
  39.9 2.2 %collective-permute-done.13.refs_14_ = bf16[80,512]{1,0:T(8,128)(2,1)S(1)} collective-permute-done((bf16[80,512]{1,0:T(8,128)(2,1)}, bf16[80,512]{1,0:T(8,128)(2,1)S(1)}, u32[]{:S(2)}, u32[]{:S(2)}) %collective-permute-start.13) | collective-permute-done | bytes 81952 | tf_op jit(solution)/shard_map/ppermute | solution.py:289
  42.1 1.8 %collective-permute-done.14.refs_15_ = bf16[80,512]{1,0:T(8,128)(2,1)S(1)} collective-permute-done((bf16[80,512]{1,0:T(8,128)(2,1)}, bf16[80,512]{1,0:T(8,128)(2,1)S(1)}, u32[]{:S(2)}, u32[]{:S(2)}) %collective-permute-start.14) | collective-permute-done | bytes 81952 | tf_op jit(solution)/shard_map/ppermute | solution.py:289
  43.9 5.6 %attend.1 = (bf16[128,4096]{1,0:T(8,128)(2,1)}, bf16[16,8,1024]{2,1,0:T(8,128)(2,1)}) custom-call(s32[8,128]{1,0:T(8,128)S(1)} %get-tuple-element.24.order_vmem, bf16[4,1024,128]{2,1,0:T(8,128)(2,1)S(1)} %get-tuple-element.25.rot_ref, f32[8,512]{1,0:T(8,128)S(1)} %get-tuple-element.26.bias_ref, bf16[128,1024]{1,0:T(8,128)(2,1)S(1)} %get-tuple-element.27.new_ref, ...), custom_call_target="tpu_custom_call" | custom-call | tf_op jit(solution)/shard_map/attend/pallas_call | solution.py:247
  (21 shorter events, 0.0 us)
Async XLA Ops:
  0.6 29.4 %copy-start = (bf16[1,128,4096]{2,1,0:T(8,128)(2,1)S(1)}, bf16[1,128,4096]{2,1,0:T(8,128)(2,1)}, u32[]{:S(2)}) copy-start(bf16[1,128,4096]{2,1,0:T(8,128)(2,1)} %param.7) | copy-start | bytes 3145732
  0.6 29.4 %copy-start.1 = (bf16[1,128,1024]{2,1,0:T(8,128)(2,1)S(1)}, bf16[1,128,1024]{2,1,0:T(8,128)(2,1)}, u32[]{:S(2)}) copy-start(bf16[1,128,1024]{2,1,0:T(8,128)(2,1)} %param.8) | copy-start | bytes 786436
  4.0 4.3 %collective-permute-start = (bf16[80,512]{1,0:T(8,128)(2,1)}, bf16[80,512]{1,0:T(8,128)(2,1)S(1)}, u32[]{:S(2)}, u32[]{:S(2)}) collective-permute-start(bf16[80,512]{1,0:T(8,128)(2,1)} %get-tuple-element.29), channel_id=1, source_target_pairs={{0,1},{1,0},{2,3},{3,2},{4,5},{5,4},{6,7},{7,6},{8,9},{9,8},{10,11... | collective-permute-start | bytes 245768 | tf_op jit(solution)/shard_map/ppermute | solution.py:289
  4.7 5.8 %collective-permute-start.1 = (bf16[80,512]{1,0:T(8,128)(2,1)}, bf16[80,512]{1,0:T(8,128)(2,1)S(1)}, u32[]{:S(2)}, u32[]{:S(2)}) collective-permute-start(bf16[80,512]{1,0:T(8,128)(2,1)} %get-tuple-element.30), channel_id=1, source_target_pairs={{0,2},{1,3},{2,0},{3,1},{4,6},{5,7},{6,4},{7,5},{8,10},{9,11},{10,... | collective-permute-start | bytes 245768 | tf_op jit(solution)/shard_map/ppermute | solution.py:289
  6.0 6.4 %collective-permute-start.2 = (bf16[80,512]{1,0:T(8,128)(2,1)}, bf16[80,512]{1,0:T(8,128)(2,1)S(1)}, u32[]{:S(2)}, u32[]{:S(2)}) collective-permute-start(bf16[80,512]{1,0:T(8,128)(2,1)} %get-tuple-element.31), channel_id=1, source_target_pairs={{0,3},{1,2},{2,1},{3,0},{4,7},{5,6},{6,5},{7,4},{8,11},{9,10},{10,... | collective-permute-start | bytes 245768 | tf_op jit(solution)/shard_map/ppermute | solution.py:289
  6.4 6.0 %collective-permute-start.3 = (bf16[80,512]{1,0:T(8,128)(2,1)}, bf16[80,512]{1,0:T(8,128)(2,1)S(1)}, u32[]{:S(2)}, u32[]{:S(2)}) collective-permute-start(bf16[80,512]{1,0:T(8,128)(2,1)} %get-tuple-element.32), channel_id=1, source_target_pairs={{0,4},{1,5},{2,6},{3,7},{4,0},{5,1},{6,2},{7,3},{8,12},{9,13},{10,... | collective-permute-start | bytes 245768 | tf_op jit(solution)/shard_map/ppermute | solution.py:289
  7.7 6.4 %collective-permute-start.4 = (bf16[80,512]{1,0:T(8,128)(2,1)}, bf16[80,512]{1,0:T(8,128)(2,1)S(1)}, u32[]{:S(2)}, u32[]{:S(2)}) collective-permute-start(bf16[80,512]{1,0:T(8,128)(2,1)} %get-tuple-element.33), channel_id=1, source_target_pairs={{0,5},{1,4},{2,7},{3,6},{4,1},{5,0},{6,3},{7,2},{8,13},{9,12},{10,... | collective-permute-start | bytes 245768 | tf_op jit(solution)/shard_map/ppermute | solution.py:289
  8.2 7.2 %collective-permute-start.5 = (bf16[80,512]{1,0:T(8,128)(2,1)}, bf16[80,512]{1,0:T(8,128)(2,1)S(1)}, u32[]{:S(2)}, u32[]{:S(2)}) collective-permute-start(bf16[80,512]{1,0:T(8,128)(2,1)} %get-tuple-element.34), channel_id=1, source_target_pairs={{0,6},{1,7},{2,4},{3,5},{4,2},{5,3},{6,0},{7,1},{8,14},{9,15},{10,... | collective-permute-start | bytes 245768 | tf_op jit(solution)/shard_map/ppermute | solution.py:289
  10.5 8.1 %collective-permute-start.6 = (bf16[80,512]{1,0:T(8,128)(2,1)}, bf16[80,512]{1,0:T(8,128)(2,1)S(1)}, u32[]{:S(2)}, u32[]{:S(2)}) collective-permute-start(bf16[80,512]{1,0:T(8,128)(2,1)} %get-tuple-element.35), channel_id=1, source_target_pairs={{0,7},{1,6},{2,5},{3,4},{4,3},{5,2},{6,1},{7,0},{8,15},{9,14},{10,... | collective-permute-start | bytes 245768 | tf_op jit(solution)/shard_map/ppermute | solution.py:289
  12.4 17.7 %copy-start.3 = (s32[16,16]{1,0:T(8,128)S(1)}, s32[16,16]{1,0:T(8,128)}, u32[]{:S(2)}) copy-start(s32[16,16]{1,0:T(8,128)} %stripe_ref.1) | copy-start | bytes 3076
  12.4 6.5 %collective-permute-start.7 = (bf16[80,512]{1,0:T(8,128)(2,1)}, bf16[80,512]{1,0:T(8,128)(2,1)S(1)}, u32[]{:S(2)}, u32[]{:S(2)}) collective-permute-start(bf16[80,512]{1,0:T(8,128)(2,1)} %get-tuple-element.36), channel_id=1, source_target_pairs={{0,8},{1,9},{2,10},{3,11},{4,12},{5,13},{6,14},{7,15},{8,0},{9,1},... | collective-permute-start | bytes 245768 | tf_op jit(solution)/shard_map/ppermute | solution.py:289
  12.5 13.3 %collective-permute-start.8 = (bf16[80,512]{1,0:T(8,128)(2,1)}, bf16[80,512]{1,0:T(8,128)(2,1)S(1)}, u32[]{:S(2)}, u32[]{:S(2)}) collective-permute-start(bf16[80,512]{1,0:T(8,128)(2,1)} %get-tuple-element.37), channel_id=1, source_target_pairs={{0,9},{1,8},{2,11},{3,10},{4,13},{5,12},{6,15},{7,14},{8,1},{9,0},... | collective-permute-start | bytes 245768 | tf_op jit(solution)/shard_map/ppermute | solution.py:289
  14.1 13.3 %collective-permute-start.9 = (bf16[80,512]{1,0:T(8,128)(2,1)}, bf16[80,512]{1,0:T(8,128)(2,1)S(1)}, u32[]{:S(2)}, u32[]{:S(2)}) collective-permute-start(bf16[80,512]{1,0:T(8,128)(2,1)} %get-tuple-element.38), channel_id=1, source_target_pairs={{0,10},{1,11},{2,8},{3,9},{4,14},{5,15},{6,12},{7,13},{8,2},{9,3},... | collective-permute-start | bytes 245768 | tf_op jit(solution)/shard_map/ppermute | solution.py:289
  15.4 16.4 %collective-permute-start.10 = (bf16[80,512]{1,0:T(8,128)(2,1)}, bf16[80,512]{1,0:T(8,128)(2,1)S(1)}, u32[]{:S(2)}, u32[]{:S(2)}) collective-permute-start(bf16[80,512]{1,0:T(8,128)(2,1)} %get-tuple-element.39), channel_id=1, source_target_pairs={{0,11},{1,10},{2,9},{3,8},{4,15},{5,14},{6,13},{7,12},{8,3},{9,2},... | collective-permute-start | bytes 245768 | tf_op jit(solution)/shard_map/ppermute | solution.py:289
  18.6 19.1 %collective-permute-start.11 = (bf16[80,512]{1,0:T(8,128)(2,1)}, bf16[80,512]{1,0:T(8,128)(2,1)S(1)}, u32[]{:S(2)}, u32[]{:S(2)}) collective-permute-start(bf16[80,512]{1,0:T(8,128)(2,1)} %get-tuple-element.40), channel_id=1, source_target_pairs={{0,12},{1,13},{2,14},{3,15},{4,8},{5,9},{6,10},{7,11},{8,4},{9,5},... | collective-permute-start | bytes 245768 | tf_op jit(solution)/shard_map/ppermute | solution.py:289
  18.9 21.0 %collective-permute-start.12 = (bf16[80,512]{1,0:T(8,128)(2,1)}, bf16[80,512]{1,0:T(8,128)(2,1)S(1)}, u32[]{:S(2)}, u32[]{:S(2)}) collective-permute-start(bf16[80,512]{1,0:T(8,128)(2,1)} %get-tuple-element.41), channel_id=1, source_target_pairs={{0,13},{1,12},{2,15},{3,14},{4,9},{5,8},{6,11},{7,10},{8,5},{9,4},... | collective-permute-start | bytes 245768 | tf_op jit(solution)/shard_map/ppermute | solution.py:289
  25.8 16.3 %collective-permute-start.13 = (bf16[80,512]{1,0:T(8,128)(2,1)}, bf16[80,512]{1,0:T(8,128)(2,1)S(1)}, u32[]{:S(2)}, u32[]{:S(2)}) collective-permute-start(bf16[80,512]{1,0:T(8,128)(2,1)} %get-tuple-element.42), channel_id=1, source_target_pairs={{0,14},{1,15},{2,12},{3,13},{4,10},{5,11},{6,8},{7,9},{8,6},{9,7},... | collective-permute-start | bytes 245768 | tf_op jit(solution)/shard_map/ppermute | solution.py:289
  27.4 2.7 %copy-start.4 = (s32[16]{0:T(128)S(1)}, s32[16]{0:T(128)}, u32[]{:S(2)}) copy-start(s32[16]{0:T(128)} %assign_any.1) | copy-start | bytes 196
  27.4 2.7 %copy-start.5 = (s32[16]{0:T(128)S(1)}, s32[16]{0:T(128)}, u32[]{:S(2)}) copy-start(s32[16]{0:T(128)} %length_any.1) | copy-start | bytes 196
  27.4 16.4 %collective-permute-start.14 = (bf16[80,512]{1,0:T(8,128)(2,1)}, bf16[80,512]{1,0:T(8,128)(2,1)S(1)}, u32[]{:S(2)}, u32[]{:S(2)}) collective-permute-start(bf16[80,512]{1,0:T(8,128)(2,1)} %get-tuple-element.43), channel_id=1, source_target_pairs={{0,15},{1,14},{2,13},{3,12},{4,11},{5,10},{6,9},{7,8},{8,7},{9,6},... | collective-permute-start | bytes 245768 | tf_op jit(solution)/shard_map/ppermute | solution.py:289
  30.1 13.8 %copy-start.2 = (bf16[80,512]{1,0:T(8,128)(2,1)S(1)}, bf16[80,512]{1,0:T(8,128)(2,1)}, u32[]{:S(2)}) copy-start(bf16[80,512]{1,0:T(8,128)(2,1)} %get-tuple-element.28.refs_0_) | copy-start | bytes 245764

commit v3 on v2

--- a/solution.py
+++ b/solution.py
@@ -283,10 +283,13 @@
 
 
 def exchange(blocks):
-    got = [blocks[0]]
-    for t in range(len(blocks) - 1, 0, -1):
+    got = list(blocks)
+    half = len(blocks) // 2
+    far, near = list(range(half, 2 * half)), list(range(half - 1, 0, -1))
+    order = [t for pair in zip(far, near + [None]) for t in pair if t is not None]
+    for t in order:
         pairs = [(source, source ^ t) for source in range(len(blocks))]
-        got.insert(1, lax.ppermute(blocks[t], "pg", pairs))
+        got[t] = lax.ppermute(blocks[t], "pg", pairs)
     return got
 
 

time: 49.7 us -> 49.7 us (level)
  no operation moved by 1% of the time
where the time goes in v3:
time: 49.7 us; the launch traced here: 49.5 us
  starting transfers between devices  25.4 us (51%)
  waiting for transfers between devices  12.7 us (26%)
  Pallas kernels  10.7 us (22%)
  between operations  0.71 us (1%)
    ppermute x15, starting transfers between devices, exchange(): got[t] = lax.ppermute(blocks[t], 'pg', pairs)  25.4 us
    ppermute x15, waiting for transfers between devices, exchange(): got[t] = lax.ppermute(blocks[t], 'pg', pairs)  12.7 us
    pallas_call x1, Pallas kernels, attend(): pl.pallas_call(functools.partial(attend_kernel, count > 0, len(got)), out...  5.64 us
    pallas_call x1, Pallas kernels, front(): pl.pallas_call(front_kernel, out_shape=[jax.ShapeDtypeStruct((2 * slots +...  3.32 us
    pallas_call x1, Pallas kernels, rotate_queries(): pl.pallas_call(query_kernel, out_shape=(jax.ShapeDtypeStruct((KV_HEADS, P...  1.69 us
  transfers between devices with their start and end apart: 15, of which 5 were waited for; matrix products, arithmetic and copies ran while one was open for 0% of the time, Pallas kernels for 3%

profile of v3, /device:TPU:19, one launch (start us, length us, event | category | flops | bytes accessed | tf_op | source)
XLA Modules:
  0.0 49.5 jit_solution(16832331248335416376)
XLA Ops:
  0.7 3.3 %front.1 = (bf16[80,512]{1,0:T(8,128)(2,1)}, bf16[80,512]{1,0:T(8,128)(2,1)}, bf16[80,512]{1,0:T(8,128)(2,1)}, bf16[80,512]{1,0:T(8,128)(2,1)}, bf16[80,512]{1,0...) custom-call(s32[1]{0:T(128)} %bitcast.me_ref, ...), custom_call_target="tpu_custom_call" | custom-call | tf_op jit(solution)/shard_map/front/pallas_call | solution.py:108
  4.0 0.7 %collective-permute-start = (bf16[80,512]{1,0:T(8,128)(2,1)}, bf16[80,512]{1,0:T(8,128)(2,1)S(1)}, u32[]{:S(2)}, u32[]{:S(2)}) collective-permute-start(bf16[80,512]{1,0:T(8,128)(2,1)} %get-tuple-element.29), channel_id=1, source_target_pairs={{0,1},{1,0},{2,3},{3,2},{4,5},{5,4},{6,7},{7,6},{8,9},{9,8},{10,11... | collective-permute-start | bytes 245768 | tf_op jit(solution)/shard_map/ppermute | solution.py:292
  4.7 1.3 %collective-permute-start.1 = (bf16[80,512]{1,0:T(8,128)(2,1)}, bf16[80,512]{1,0:T(8,128)(2,1)S(1)}, u32[]{:S(2)}, u32[]{:S(2)}) collective-permute-start(bf16[80,512]{1,0:T(8,128)(2,1)} %get-tuple-element.30), channel_id=1, source_target_pairs={{0,2},{1,3},{2,0},{3,1},{4,6},{5,7},{6,4},{7,5},{8,10},{9,11},{10,... | collective-permute-start | bytes 245768 | tf_op jit(solution)/shard_map/ppermute | solution.py:292
  6.0 0.5 collective-permute-start.2
  6.4 1.3 %collective-permute-start.3 = (bf16[80,512]{1,0:T(8,128)(2,1)}, bf16[80,512]{1,0:T(8,128)(2,1)S(1)}, u32[]{:S(2)}, u32[]{:S(2)}) collective-permute-start(bf16[80,512]{1,0:T(8,128)(2,1)} %get-tuple-element.32), channel_id=1, source_target_pairs={{0,4},{1,5},{2,6},{3,7},{4,0},{5,1},{6,2},{7,3},{8,12},{9,13},{10,... | collective-permute-start | bytes 245768 | tf_op jit(solution)/shard_map/ppermute | solution.py:292
  7.7 0.5 %collective-permute-start.4 = (bf16[80,512]{1,0:T(8,128)(2,1)}, bf16[80,512]{1,0:T(8,128)(2,1)S(1)}, u32[]{:S(2)}, u32[]{:S(2)}) collective-permute-start(bf16[80,512]{1,0:T(8,128)(2,1)} %get-tuple-element.33), channel_id=1, source_target_pairs={{0,5},{1,4},{2,7},{3,6},{4,1},{5,0},{6,3},{7,2},{8,13},{9,12},{10,... | collective-permute-start | bytes 245768 | tf_op jit(solution)/shard_map/ppermute | solution.py:292
  8.2 2.3 %collective-permute-start.5 = (bf16[80,512]{1,0:T(8,128)(2,1)}, bf16[80,512]{1,0:T(8,128)(2,1)S(1)}, u32[]{:S(2)}, u32[]{:S(2)}) collective-permute-start(bf16[80,512]{1,0:T(8,128)(2,1)} %get-tuple-element.34), channel_id=1, source_target_pairs={{0,6},{1,7},{2,4},{3,5},{4,2},{5,3},{6,0},{7,1},{8,14},{9,15},{10,... | collective-permute-start | bytes 245768 | tf_op jit(solution)/shard_map/ppermute | solution.py:292
  10.5 1.9 %collective-permute-start.6 = (bf16[80,512]{1,0:T(8,128)(2,1)}, bf16[80,512]{1,0:T(8,128)(2,1)S(1)}, u32[]{:S(2)}, u32[]{:S(2)}) collective-permute-start(bf16[80,512]{1,0:T(8,128)(2,1)} %get-tuple-element.35), channel_id=1, source_target_pairs={{0,7},{1,6},{2,5},{3,4},{4,3},{5,2},{6,1},{7,0},{8,15},{9,14},{10,... | collective-permute-start | bytes 245768 | tf_op jit(solution)/shard_map/ppermute | solution.py:292
  12.4 0.1 collective-permute-start.7
  12.5 1.7 %collective-permute-start.8 = (bf16[80,512]{1,0:T(8,128)(2,1)}, bf16[80,512]{1,0:T(8,128)(2,1)S(1)}, u32[]{:S(2)}, u32[]{:S(2)}) collective-permute-start(bf16[80,512]{1,0:T(8,128)(2,1)} %get-tuple-element.37), channel_id=1, source_target_pairs={{0,9},{1,8},{2,11},{3,10},{4,13},{5,12},{6,15},{7,14},{8,1},{9,0},... | collective-permute-start | bytes 245768 | tf_op jit(solution)/shard_map/ppermute | solution.py:292
  14.1 0.7 %collective-permute-start.9 = (bf16[80,512]{1,0:T(8,128)(2,1)}, bf16[80,512]{1,0:T(8,128)(2,1)S(1)}, u32[]{:S(2)}, u32[]{:S(2)}) collective-permute-start(bf16[80,512]{1,0:T(8,128)(2,1)} %get-tuple-element.38), channel_id=1, source_target_pairs={{0,10},{1,11},{2,8},{3,9},{4,14},{5,15},{6,12},{7,13},{8,2},{9,3},... | collective-permute-start | bytes 245768 | tf_op jit(solution)/shard_map/ppermute | solution.py:292
  14.8 0.6 %collective-permute-done.5.refs_6_ = bf16[80,512]{1,0:T(8,128)(2,1)S(1)} collective-permute-done((bf16[80,512]{1,0:T(8,128)(2,1)}, bf16[80,512]{1,0:T(8,128)(2,1)S(1)}, u32[]{:S(2)}, u32[]{:S(2)}) %collective-permute-start.5) | collective-permute-done | bytes 81952 | tf_op jit(solution)/shard_map/ppermute | solution.py:292
  15.4 3.2 %collective-permute-start.10 = (bf16[80,512]{1,0:T(8,128)(2,1)}, bf16[80,512]{1,0:T(8,128)(2,1)S(1)}, u32[]{:S(2)}, u32[]{:S(2)}) collective-permute-start(bf16[80,512]{1,0:T(8,128)(2,1)} %get-tuple-element.39), channel_id=1, source_target_pairs={{0,11},{1,10},{2,9},{3,8},{4,15},{5,14},{6,13},{7,12},{8,3},{9,2},... | collective-permute-start | bytes 245768 | tf_op jit(solution)/shard_map/ppermute | solution.py:292
  18.6 0.3 collective-permute-start.11
  18.9 6.9 %collective-permute-start.12 = (bf16[80,512]{1,0:T(8,128)(2,1)}, bf16[80,512]{1,0:T(8,128)(2,1)S(1)}, u32[]{:S(2)}, u32[]{:S(2)}) collective-permute-start(bf16[80,512]{1,0:T(8,128)(2,1)} %get-tuple-element.41), channel_id=1, source_target_pairs={{0,13},{1,12},{2,15},{3,14},{4,9},{5,8},{6,11},{7,10},{8,5},{9,4},... | collective-permute-start | bytes 245768 | tf_op jit(solution)/shard_map/ppermute | solution.py:292
  25.8 1.6 %collective-permute-start.13 = (bf16[80,512]{1,0:T(8,128)(2,1)}, bf16[80,512]{1,0:T(8,128)(2,1)S(1)}, u32[]{:S(2)}, u32[]{:S(2)}) collective-permute-start(bf16[80,512]{1,0:T(8,128)(2,1)} %get-tuple-element.42), channel_id=1, source_target_pairs={{0,14},{1,15},{2,12},{3,13},{4,10},{5,11},{6,8},{7,9},{8,6},{9,7},... | collective-permute-start | bytes 245768 | tf_op jit(solution)/shard_map/ppermute | solution.py:292
  27.4 2.7 %collective-permute-start.14 = (bf16[80,512]{1,0:T(8,128)(2,1)}, bf16[80,512]{1,0:T(8,128)(2,1)S(1)}, u32[]{:S(2)}, u32[]{:S(2)}) collective-permute-start(bf16[80,512]{1,0:T(8,128)(2,1)} %get-tuple-element.43), channel_id=1, source_target_pairs={{0,15},{1,14},{2,13},{3,12},{4,11},{5,10},{6,9},{7,8},{8,7},{9,6},... | collective-permute-start | bytes 245768 | tf_op jit(solution)/shard_map/ppermute | solution.py:292
  30.1 0.0 copy-start.2
  30.1 1.7 %rotate_queries.1 = (bf16[4,1024,128]{2,1,0:T(8,128)(2,1)S(1)}, f32[8,512]{1,0:T(8,128)S(1)}, bf16[128,1024]{1,0:T(8,128)(2,1)S(1)}, s32[8,128]{1,0:T(8,128)S(1)}) custom-call(s32[1]{0:T(128)} %bitcast.me_ref, s32[16]{0:T(128)S(1)} %copy-done.4, s32[16]{0:T(128)S(1)} %copy-done.5, s32[16,16]{1,0:T(8,128)S(1)} %copy-done.3, bf16[128,4096]{1,0:T(8,128)(2,1)S(1)} %bitcast.6, ...), custom_call_target="tpu_custom_call" | custom-call | tf_op jit(solution)/shard_map/rotate_queries/pallas_call | solution.py:161
  31.8 5.9 %collective-permute-done.11.refs_12_ = bf16[80,512]{1,0:T(8,128)(2,1)S(1)} collective-permute-done((bf16[80,512]{1,0:T(8,128)(2,1)}, bf16[80,512]{1,0:T(8,128)(2,1)S(1)}, u32[]{:S(2)}, u32[]{:S(2)}) %collective-permute-start.11) | collective-permute-done | bytes 81952 | tf_op jit(solution)/shard_map/ppermute | solution.py:292
  37.7 2.2 %collective-permute-done.12.refs_13_ = bf16[80,512]{1,0:T(8,128)(2,1)S(1)} collective-permute-done((bf16[80,512]{1,0:T(8,128)(2,1)}, bf16[80,512]{1,0:T(8,128)(2,1)S(1)}, u32[]{:S(2)}, u32[]{:S(2)}) %collective-permute-start.12) | collective-permute-done | bytes 81952 | tf_op jit(solution)/shard_map/ppermute | solution.py:292
  39.9 2.2 %collective-permute-done.13.refs_14_ = bf16[80,512]{1,0:T(8,128)(2,1)S(1)} collective-permute-done((bf16[80,512]{1,0:T(8,128)(2,1)}, bf16[80,512]{1,0:T(8,128)(2,1)S(1)}, u32[]{:S(2)}, u32[]{:S(2)}) %collective-permute-start.13) | collective-permute-done | bytes 81952 | tf_op jit(solution)/shard_map/ppermute | solution.py:292
  42.1 1.8 %collective-permute-done.14.refs_15_ = bf16[80,512]{1,0:T(8,128)(2,1)S(1)} collective-permute-done((bf16[80,512]{1,0:T(8,128)(2,1)}, bf16[80,512]{1,0:T(8,128)(2,1)S(1)}, u32[]{:S(2)}, u32[]{:S(2)}) %collective-permute-start.14) | collective-permute-done | bytes 81952 | tf_op jit(solution)/shard_map/ppermute | solution.py:292
  43.9 5.6 %attend.1 = (bf16[128,4096]{1,0:T(8,128)(2,1)}, bf16[16,8,1024]{2,1,0:T(8,128)(2,1)}) custom-call(s32[8,128]{1,0:T(8,128)S(1)} %get-tuple-element.24.order_vmem, bf16[4,1024,128]{2,1,0:T(8,128)(2,1)S(1)} %get-tuple-element.25.rot_ref, f32[8,512]{1,0:T(8,128)S(1)} %get-tuple-element.26.bias_ref, bf16[128,1024]{1,0:T(8,128)(2,1)S(1)} %get-tuple-element.27.new_ref, ...), custom_call_target="tpu_custom_call" | custom-call | tf_op jit(solution)/shard_map/attend/pallas_call | solution.py:247
  (21 shorter events, 0.0 us)
Async XLA Ops:
  0.6 29.4 %copy-start = (bf16[1,128,4096]{2,1,0:T(8,128)(2,1)S(1)}, bf16[1,128,4096]{2,1,0:T(8,128)(2,1)}, u32[]{:S(2)}) copy-start(bf16[1,128,4096]{2,1,0:T(8,128)(2,1)} %param.7) | copy-start | bytes 3145732
  0.6 29.4 %copy-start.1 = (bf16[1,128,1024]{2,1,0:T(8,128)(2,1)S(1)}, bf16[1,128,1024]{2,1,0:T(8,128)(2,1)}, u32[]{:S(2)}) copy-start(bf16[1,128,1024]{2,1,0:T(8,128)(2,1)} %param.8) | copy-start | bytes 786436
  4.0 4.3 %collective-permute-start = (bf16[80,512]{1,0:T(8,128)(2,1)}, bf16[80,512]{1,0:T(8,128)(2,1)S(1)}, u32[]{:S(2)}, u32[]{:S(2)}) collective-permute-start(bf16[80,512]{1,0:T(8,128)(2,1)} %get-tuple-element.29), channel_id=1, source_target_pairs={{0,1},{1,0},{2,3},{3,2},{4,5},{5,4},{6,7},{7,6},{8,9},{9,8},{10,11... | collective-permute-start | bytes 245768 | tf_op jit(solution)/shard_map/ppermute | solution.py:292
  4.7 5.8 %collective-permute-start.1 = (bf16[80,512]{1,0:T(8,128)(2,1)}, bf16[80,512]{1,0:T(8,128)(2,1)S(1)}, u32[]{:S(2)}, u32[]{:S(2)}) collective-permute-start(bf16[80,512]{1,0:T(8,128)(2,1)} %get-tuple-element.30), channel_id=1, source_target_pairs={{0,2},{1,3},{2,0},{3,1},{4,6},{5,7},{6,4},{7,5},{8,10},{9,11},{10,... | collective-permute-start | bytes 245768 | tf_op jit(solution)/shard_map/ppermute | solution.py:292
  6.0 6.4 %collective-permute-start.2 = (bf16[80,512]{1,0:T(8,128)(2,1)}, bf16[80,512]{1,0:T(8,128)(2,1)S(1)}, u32[]{:S(2)}, u32[]{:S(2)}) collective-permute-start(bf16[80,512]{1,0:T(8,128)(2,1)} %get-tuple-element.31), channel_id=1, source_target_pairs={{0,3},{1,2},{2,1},{3,0},{4,7},{5,6},{6,5},{7,4},{8,11},{9,10},{10,... | collective-permute-start | bytes 245768 | tf_op jit(solution)/shard_map/ppermute | solution.py:292
  6.4 6.0 %collective-permute-start.3 = (bf16[80,512]{1,0:T(8,128)(2,1)}, bf16[80,512]{1,0:T(8,128)(2,1)S(1)}, u32[]{:S(2)}, u32[]{:S(2)}) collective-permute-start(bf16[80,512]{1,0:T(8,128)(2,1)} %get-tuple-element.32), channel_id=1, source_target_pairs={{0,4},{1,5},{2,6},{3,7},{4,0},{5,1},{6,2},{7,3},{8,12},{9,13},{10,... | collective-permute-start | bytes 245768 | tf_op jit(solution)/shard_map/ppermute | solution.py:292
  7.7 6.4 %collective-permute-start.4 = (bf16[80,512]{1,0:T(8,128)(2,1)}, bf16[80,512]{1,0:T(8,128)(2,1)S(1)}, u32[]{:S(2)}, u32[]{:S(2)}) collective-permute-start(bf16[80,512]{1,0:T(8,128)(2,1)} %get-tuple-element.33), channel_id=1, source_target_pairs={{0,5},{1,4},{2,7},{3,6},{4,1},{5,0},{6,3},{7,2},{8,13},{9,12},{10,... | collective-permute-start | bytes 245768 | tf_op jit(solution)/shard_map/ppermute | solution.py:292
  8.2 7.2 %collective-permute-start.5 = (bf16[80,512]{1,0:T(8,128)(2,1)}, bf16[80,512]{1,0:T(8,128)(2,1)S(1)}, u32[]{:S(2)}, u32[]{:S(2)}) collective-permute-start(bf16[80,512]{1,0:T(8,128)(2,1)} %get-tuple-element.34), channel_id=1, source_target_pairs={{0,6},{1,7},{2,4},{3,5},{4,2},{5,3},{6,0},{7,1},{8,14},{9,15},{10,... | collective-permute-start | bytes 245768 | tf_op jit(solution)/shard_map/ppermute | solution.py:292
  10.5 8.1 %collective-permute-start.6 = (bf16[80,512]{1,0:T(8,128)(2,1)}, bf16[80,512]{1,0:T(8,128)(2,1)S(1)}, u32[]{:S(2)}, u32[]{:S(2)}) collective-permute-start(bf16[80,512]{1,0:T(8,128)(2,1)} %get-tuple-element.35), channel_id=1, source_target_pairs={{0,7},{1,6},{2,5},{3,4},{4,3},{5,2},{6,1},{7,0},{8,15},{9,14},{10,... | collective-permute-start | bytes 245768 | tf_op jit(solution)/shard_map/ppermute | solution.py:292
  12.4 17.7 %copy-start.3 = (s32[16,16]{1,0:T(8,128)S(1)}, s32[16,16]{1,0:T(8,128)}, u32[]{:S(2)}) copy-start(s32[16,16]{1,0:T(8,128)} %stripe_ref.1) | copy-start | bytes 3076
  12.4 6.5 %collective-permute-start.7 = (bf16[80,512]{1,0:T(8,128)(2,1)}, bf16[80,512]{1,0:T(8,128)(2,1)S(1)}, u32[]{:S(2)}, u32[]{:S(2)}) collective-permute-start(bf16[80,512]{1,0:T(8,128)(2,1)} %get-tuple-element.36), channel_id=1, source_target_pairs={{0,8},{1,9},{2,10},{3,11},{4,12},{5,13},{6,14},{7,15},{8,0},{9,1},... | collective-permute-start | bytes 245768 | tf_op jit(solution)/shard_map/ppermute | solution.py:292
  12.5 13.3 %collective-permute-start.8 = (bf16[80,512]{1,0:T(8,128)(2,1)}, bf16[80,512]{1,0:T(8,128)(2,1)S(1)}, u32[]{:S(2)}, u32[]{:S(2)}) collective-permute-start(bf16[80,512]{1,0:T(8,128)(2,1)} %get-tuple-element.37), channel_id=1, source_target_pairs={{0,9},{1,8},{2,11},{3,10},{4,13},{5,12},{6,15},{7,14},{8,1},{9,0},... | collective-permute-start | bytes 245768 | tf_op jit(solution)/shard_map/ppermute | solution.py:292
  14.1 13.3 %collective-permute-start.9 = (bf16[80,512]{1,0:T(8,128)(2,1)}, bf16[80,512]{1,0:T(8,128)(2,1)S(1)}, u32[]{:S(2)}, u32[]{:S(2)}) collective-permute-start(bf16[80,512]{1,0:T(8,128)(2,1)} %get-tuple-element.38), channel_id=1, source_target_pairs={{0,10},{1,11},{2,8},{3,9},{4,14},{5,15},{6,12},{7,13},{8,2},{9,3},... | collective-permute-start | bytes 245768 | tf_op jit(solution)/shard_map/ppermute | solution.py:292
  15.4 16.4 %collective-permute-start.10 = (bf16[80,512]{1,0:T(8,128)(2,1)}, bf16[80,512]{1,0:T(8,128)(2,1)S(1)}, u32[]{:S(2)}, u32[]{:S(2)}) collective-permute-start(bf16[80,512]{1,0:T(8,128)(2,1)} %get-tuple-element.39), channel_id=1, source_target_pairs={{0,11},{1,10},{2,9},{3,8},{4,15},{5,14},{6,13},{7,12},{8,3},{9,2},... | collective-permute-start | bytes 245768 | tf_op jit(solution)/shard_map/ppermute | solution.py:292
  18.6 19.1 %collective-permute-start.11 = (bf16[80,512]{1,0:T(8,128)(2,1)}, bf16[80,512]{1,0:T(8,128)(2,1)S(1)}, u32[]{:S(2)}, u32[]{:S(2)}) collective-permute-start(bf16[80,512]{1,0:T(8,128)(2,1)} %get-tuple-element.40), channel_id=1, source_target_pairs={{0,12},{1,13},{2,14},{3,15},{4,8},{5,9},{6,10},{7,11},{8,4},{9,5},... | collective-permute-start | bytes 245768 | tf_op jit(solution)/shard_map/ppermute | solution.py:292
  18.9 21.0 %collective-permute-start.12 = (bf16[80,512]{1,0:T(8,128)(2,1)}, bf16[80,512]{1,0:T(8,128)(2,1)S(1)}, u32[]{:S(2)}, u32[]{:S(2)}) collective-permute-start(bf16[80,512]{1,0:T(8,128)(2,1)} %get-tuple-element.41), channel_id=1, source_target_pairs={{0,13},{1,12},{2,15},{3,14},{4,9},{5,8},{6,11},{7,10},{8,5},{9,4},... | collective-permute-start | bytes 245768 | tf_op jit(solution)/shard_map/ppermute | solution.py:292
  25.8 16.3 %collective-permute-start.13 = (bf16[80,512]{1,0:T(8,128)(2,1)}, bf16[80,512]{1,0:T(8,128)(2,1)S(1)}, u32[]{:S(2)}, u32[]{:S(2)}) collective-permute-start(bf16[80,512]{1,0:T(8,128)(2,1)} %get-tuple-element.42), channel_id=1, source_target_pairs={{0,14},{1,15},{2,12},{3,13},{4,10},{5,11},{6,8},{7,9},{8,6},{9,7},... | collective-permute-start | bytes 245768 | tf_op jit(solution)/shard_map/ppermute | solution.py:292
  27.4 2.7 %copy-start.4 = (s32[16]{0:T(128)S(1)}, s32[16]{0:T(128)}, u32[]{:S(2)}) copy-start(s32[16]{0:T(128)} %assign_any.1) | copy-start | bytes 196
  27.4 2.7 %copy-start.5 = (s32[16]{0:T(128)S(1)}, s32[16]{0:T(128)}, u32[]{:S(2)}) copy-start(s32[16]{0:T(128)} %length_any.1) | copy-start | bytes 196
  27.4 16.4 %collective-permute-start.14 = (bf16[80,512]{1,0:T(8,128)(2,1)}, bf16[80,512]{1,0:T(8,128)(2,1)S(1)}, u32[]{:S(2)}, u32[]{:S(2)}) collective-permute-start(bf16[80,512]{1,0:T(8,128)(2,1)} %get-tuple-element.43), channel_id=1, source_target_pairs={{0,15},{1,14},{2,13},{3,12},{4,11},{5,10},{6,9},{7,8},{8,7},{9,6},... | collective-permute-start | bytes 245768 | tf_op jit(solution)/shard_map/ppermute | solution.py:292
  30.1 13.8 %copy-start.2 = (bf16[80,512]{1,0:T(8,128)(2,1)S(1)}, bf16[80,512]{1,0:T(8,128)(2,1)}, u32[]{:S(2)}) copy-start(bf16[80,512]{1,0:T(8,128)(2,1)} %get-tuple-element.28.refs_0_) | copy-start | bytes 245764

commit v4 on v2

v4 whole, which is shorter than its diff:
```python
import functools
import math

import jax
import jax.numpy as jnp
import numpy as np
from jax import lax
from jax.experimental import pallas as pl
from jax.experimental.pallas import tpu as pltpu
from jax.sharding import PartitionSpec as P

Q_HEADS = 32
KV_HEADS = 4
HEAD_DIM = 128
PER_KV = Q_HEADS // KV_HEADS
KV_WIDTH = KV_HEADS * HEAD_DIM
WIDTH = 2 * KV_WIDTH

ROPE_BASE = 1000000.0
MASKED = -1e30
SCALE = HEAD_DIM ** -0.5 / math.log(2.0)
CHUNK = 256
LATE = 4

SMEM = pl.BlockSpec(memory_space=pltpu.SMEM)
VMEM = pl.BlockSpec(memory_space=pltpu.VMEM)
ANY = pl.BlockSpec(memory_space=pl.ANY)


def params(mib):
    return pltpu.CompilerParams(vmem_limit_bytes=mib * 1024 * 1024)


def column(head):
    return slice(head * HEAD_DIM, (head + 1) * HEAD_DIM)


def order_of(groups):
    half = groups // 2
    far, near = list(range(half, 2 * half)), list(range(half - 1, 0, -1))
    order = [0]
    for at in range(half):
        order += far[at : at + 1] + near[at : at + 1]
    return order


def rotation_tables(rows):
    half = HEAD_DIM // 2
    freqs = np.tile(ROPE_BASE ** (-np.arange(half, dtype=np.float64) / half), 2)
    angles = np.arange(rows, dtype=np.float64)[:, None] * freqs[None, :]
    parts = [np.cos(angles), np.sin(angles), np.tile(freqs, (8, 1))]
    return jnp.asarray(np.concatenate(parts, axis=0).astype(np.float32))


def rotation(table_ref, length):
    rows = (table_ref.shape[0] - 8) // 2
    start = length.astype(jnp.float32) * table_ref[2 * rows : 2 * rows + 8, :]
    cos_start, sin_start = jnp.cos(start)[0:1], jnp.sin(start)[0:1]
    cos_row, sin_row = table_ref[0:rows, :], table_ref[rows : 2 * rows, :]
    lane = lax.broadcasted_iota(jnp.int32, (1, HEAD_DIM), 1)
    sign = jnp.where(lane < HEAD_DIM // 2, -1.0, 1.0)
    cosine = cos_row * cos_start - sin_row * sin_start
    return cosine, sin_row * (cos_start * sign) + cos_row * (sin_start * sign)


def turn(x, cosine, sine):
    x = x.astype(jnp.float32)
    return (x * cosine + pltpu.roll(x, HEAD_DIM // 2, 1) * sine).astype(jnp.bfloat16)


def front_kernel(order, me_ref, assign_any, length_any, owner_any, block_any, table_any, pool_any, *refs):
    groups, slots, width = pool_any.shape
    send_refs, refs = refs[:groups], refs[groups:]
    assign_ref, length_ref, owner_ref, residue_ref, block_ref, table_ref, rows_ref, small_sems, pool_sems = refs
    new_count = block_any.shape[0]
    count = new_count // groups
    smalls = [
        pltpu.make_async_copy(assign_any, assign_ref, small_sems.at[0]),
        pltpu.make_async_copy(length_any, length_ref, small_sems.at[1]),
        pltpu.make_async_copy(owner_any, owner_ref, small_sems.at[2]),
        pltpu.make_async_copy(block_any, block_ref, small_sems.at[3]),
        pltpu.make_async_copy(table_any, table_ref, small_sems.at[4]),
    ]
    for copy in smalls:
        copy.start()
    me = me_ref[0]
    smalls[0].wait()

    def pool_copy(p):
        return pltpu.make_async_copy(
            pool_any.at[assign_ref[me ^ order[p]]], send_refs[p].at[:, pl.ds(0, width)], pool_sems.at[p]
        )

    for p in range(groups):
        pool_copy(p).start()
    for copy in smalls[1:]:
        copy.wait()
    request = assign_ref[me]
    for residue in range(groups):
        residue_ref[owner_ref[request, residue]] = residue
    cosine, sine = rotation(table_ref, length_ref[request])
    for head in range(KV_HEADS):
        rows_ref[head] = turn(block_ref[:, column(head)], cosine, sine).astype(jnp.float32)
        rows_ref[KV_HEADS + head] = block_ref[:, column(KV_HEADS + head)].astype(jnp.float32)
    quarter = width * count // slots // HEAD_DIM
    for p in range(groups):
        residue = residue_ref[me ^ order[p]]
        for lanes in range(quarter):
            stack = [
                rows_ref[at + lanes, pl.ds(residue, count, stride=groups), :]
                for at in range(0, 2 * KV_HEADS, quarter)
            ]
            send_refs[p][:, width + lanes * HEAD_DIM : width + (lanes + 1) * HEAD_DIM] = jnp.concatenate(
                stack, axis=0
            ).astype(jnp.bfloat16)
    for p in range(groups):
        pool_copy(p).wait()


def front(order, me, assignment, prefix_len, owner_map, block_kv, table, pool):
    groups, slots, width = pool.shape
    new_count = block_kv.shape[0]
    count = new_count // groups
    block = jax.ShapeDtypeStruct((slots, width + width * count // slots), jnp.bfloat16)
    return pl.pallas_call(
        functools.partial(front_kernel, order),
        out_shape=[block] * groups,
        in_specs=[SMEM] + [ANY] * 6,
        out_specs=[VMEM] * groups,
        scratch_shapes=[
            pltpu.SMEM(assignment.shape, jnp.int32),
            pltpu.SMEM(prefix_len.shape, jnp.int32),
            pltpu.SMEM(owner_map.shape, jnp.int32),
            pltpu.SMEM(assignment.shape, jnp.int32),
            pltpu.VMEM(block_kv.shape, jnp.bfloat16),
            pltpu.VMEM(table.shape, jnp.float32),
            pltpu.VMEM((2 * KV_HEADS, new_count, HEAD_DIM), jnp.float32),
            pltpu.SemaphoreType.DMA((5,)),
            pltpu.SemaphoreType.DMA((groups,)),
        ],
        compiler_params=params(60),
        name="front",
    )(me, assignment, prefix_len, owner_map, block_kv, table, pool)


def query_kernel(
    order, me_ref, assign_ref, length_ref, stripe_ref, q_ref, block_ref, table_ref,
    rot_ref, bias_ref, new_ref, request_ref,
):
    new_count = q_ref.shape[0]
    groups = assign_ref.shape[0]
    span = bias_ref.shape[1]
    slots = span // groups
    me = me_ref[0]
    request = assign_ref[me]
    length = length_ref[request]
    lane = lax.broadcasted_iota(jnp.int32, (8, span), 1)
    piece, slot = lane // slots, lane % slots
    place = lax.broadcasted_iota(jnp.int32, request_ref.shape, 1)
    if order is None:
        holder = piece
    else:
        holder, requests = jnp.zeros_like(piece), jnp.zeros_like(place)
        for p in range(groups):
            holder = jnp.where(piece == p, me ^ order[p], holder)
            requests = jnp.where(place == p, assign_ref[me ^ order[p]], requests)
        request_ref[...] = requests

    def visit(residue, bias):
        live = (holder == stripe_ref[request, residue]) & (slot * groups + residue < length)
        return jnp.where(live, 0.0, bias)

    bias_ref[...] = lax.fori_loop(0, groups, visit, jnp.full((8, span), MASKED, jnp.float32))
    cosine, sine = rotation(table_ref, length)
    for head in range(KV_HEADS):
        new_ref[:, column(head)] = turn(block_ref[:, column(head)], cosine, sine)
    new_ref[:, KV_WIDTH:] = block_ref[:, KV_WIDTH:]
    for head in range(Q_HEADS):
        rows = slice((head % PER_KV) * new_count, (head % PER_KV + 1) * new_count)
        rot_ref[head // PER_KV, rows, :] = turn(q_ref[:, column(head)], cosine, sine)


def rotate_queries(order, me, assignment, prefix_len, stripe_map, queries, block_kv, table, span):
    new_count = queries.shape[0]
    return pl.pallas_call(
        functools.partial(query_kernel, order),
        out_shape=(
            jax.ShapeDtypeStruct((KV_HEADS, PER_KV * new_count, HEAD_DIM), jnp.bfloat16),
            jax.ShapeDtypeStruct((8, span), jnp.float32),
            jax.ShapeDtypeStruct(block_kv.shape, jnp.bfloat16),
            jax.ShapeDtypeStruct((8, HEAD_DIM), jnp.int32),
        ),
        in_specs=[SMEM, SMEM, SMEM, SMEM, VMEM, VMEM, VMEM],
        out_specs=(VMEM, VMEM, VMEM, VMEM),
        compiler_params=params(32),
        name="rotate_queries",
    )(me, assignment, prefix_len, stripe_map, queries, block_kv, table)


def attend_kernel(pieces, first, early, final, unpack, *refs):
    rot_ref, bias_ref, refs = refs[0], refs[1], refs[2:]
    if early:
        (sum_in, total_in, high_in), refs = refs[:3], refs[3:]
    else:
        new_ref, refs = refs[0], refs[1:]
    got_refs, refs = refs[:pieces], refs[pieces:]
    if unpack:
        request_vmem, refs = refs[0], refs[1:]
        if early:
            refs = refs[1:]
    if final:
        out_ref, refs = refs[0], refs[1:]
    else:
        (sum_out, total_out, high_out), refs = refs[:3], refs[3:]
    if unpack:
        (decode_ref, rows_ref, request_ref, request_sem, decode_sems), refs = refs[:5], refs[5:]
        count = rows_ref.shape[1]
        request_copy = pltpu.make_async_copy(request_vmem, request_ref, request_sem)
        request_copy.start()
    if final:
        done_ref, out_sems = refs
        new_count = done_ref.shape[1]
    else:
        new_count = rot_ref.shape[1] // PER_KV
    slots = got_refs[0].shape[0]
    span = pieces * slots
    bias = bias_ref[0:1, first * slots : first * slots + span]
    if not early:
        token = lax.broadcasted_iota(jnp.int32, (CHUNK, new_count), 0) % new_count
        causal = jnp.where(lax.broadcasted_iota(jnp.int32, (CHUNK, new_count), 1) <= token, 0.0, MASKED)
    per_head = PER_KV * new_count // CHUNK
    keys, values = {}, {}

    def scores_of(at):
        head, chunk = divmod(at, per_head)
        if chunk == 0:
            key_parts = [got[:, column(head)] for got in got_refs]
            value_parts = [got[:, column(KV_HEADS + head)] for got in got_refs]
            if not early:
                key_parts.append(new_ref[:, column(head)])
                value_parts.append(new_ref[:, column(KV_HEADS + head)])
            keys[head] = jnp.concatenate(key_parts, axis=0)
            value = jnp.concatenate(value_parts, axis=0)
            values[head] = jnp.concatenate([value, jnp.ones_like(value)], axis=1)
        query = rot_ref[head, chunk * CHUNK : (chunk + 1) * CHUNK, :]
        return lax.dot_general(query, keys[head], (((1,), (1,)), ((), ())), preferred_element_type=jnp.float32)

    def out_copy(head):
        width = PER_KV * HEAD_DIM
        return pltpu.make_async_copy(
            done_ref.at[head], out_ref.at[:, pl.ds(head * width, width)], out_sems.at[head]
        )

    def decode_copy(p):
        return pltpu.make_async_copy(
            rows_ref.at[p], decode_ref.at[request_ref[0, first + p]], decode_sems.at[p]
        )

    total_chunks = KV_HEADS * per_head
    ahead = scores_of(0)
    for at in range(total_chunks):
        scores = ahead
        if at + 1 < total_chunks:
            ahead = scores_of(at + 1)
        head, chunk = divmod(at, per_head)
        rows = slice(chunk * CHUNK, (chunk + 1) * CHUNK)
        if early:
            scores = scores * SCALE + bias
        else:
            scores = jnp.concatenate([scores[:, :span] * SCALE + bias, scores[:, span:] * SCALE + causal], axis=1)
        high = jnp.max(scores, axis=1, keepdims=True)
        if early:
            high_before = high_in[head, rows, :]
            high_joint = jnp.maximum(high_before, high)
            factor = jnp.exp2(high_before - high_joint)
            high = high_joint[:, 0:1]
        weights = jnp.exp2(scores - high).astype(jnp.bfloat16)
        summed = jnp.dot(weights, values[head], preferred_element_type=jnp.float32)
        summed, total = summed[:, :HEAD_DIM], summed[:, HEAD_DIM:]
        if early:
            summed = summed + sum_in[head, rows, :] * factor
            total = total + total_in[head, rows, :] * factor
        if final:
            result = (summed / total).astype(jnp.bfloat16)
            for row in range(CHUNK // new_count):
                done_ref[head, :, column(chunk * (CHUNK // new_count) + row)] = result[
                    row * new_count : (row + 1) * new_count
                ]
            if chunk == per_head - 1:
                out_copy(head).start()
        else:
            sum_out[head, rows, :] = summed
            total_out[head, rows, :] = total
            high_out[head, rows, :] = jnp.broadcast_to(high, (CHUNK, HEAD_DIM))
        if unpack and at == per_head - 1:
            request_copy.wait()
            for p, got in enumerate(got_refs):
                stack = got[:, WIDTH:]
                quarter = stack.shape[1]
                for part in range(slots // count):
                    rows_ref[p, :, part * quarter : (part + 1) * quarter] = stack[
                        part * count : (part + 1) * count
                    ]
                decode_copy(p).start()
    if unpack:
        for p in range(pieces):
            decode_copy(p).wait()
    if final:
        for head in range(KV_HEADS):
            out_copy(head).wait()


def attend(rot, bias, new_kv, got, first=0, sums=None, final=True, requests=None, decode=None):
    rows = rot.shape[1]
    new_count = rows // PER_KV
    pieces = len(got)
    early, unpack = sums is not None, requests is not None
    operands = [rot, bias] + (list(sums) if early else [new_kv]) + list(got)
    specs = [VMEM] * len(operands)
    shapes, out_specs, scratch, aliases = [], [], [], {}
    if unpack:
        operands.append(requests)
        specs.append(VMEM)
        if early:
            operands.append(decode)
            specs.append(ANY)
            aliases = {len(operands) - 1: 1 if final else 3}
    if final:
        shapes.append(jax.ShapeDtypeStruct((new_count, Q_HEADS * HEAD_DIM), jnp.bfloat16))
        out_specs.append(ANY)
    else:
        shapes += [jax.ShapeDtypeStruct((KV_HEADS, rows, HEAD_DIM), jnp.float32)] * 3
        out_specs += [VMEM] * 3
    if unpack:
        slots = got[0].shape[0]
        count = (got[0].shape[1] - WIDTH) * slots // WIDTH
        shapes.append(jax.ShapeDtypeStruct((new_count // count, count, WIDTH), jnp.bfloat16))
        out_specs.append(ANY)
        scratch += [
            pltpu.VMEM((pieces, count, WIDTH), jnp.bfloat16),
            pltpu.SMEM(requests.shape, jnp.int32),
            pltpu.SemaphoreType.DMA,
            pltpu.SemaphoreType.DMA((pieces,)),
        ]
    if final:
        scratch += [
            pltpu.VMEM((KV_HEADS, new_count, PER_KV * HEAD_DIM), jnp.bfloat16),
            pltpu.SemaphoreType.DMA((KV_HEADS,)),
        ]
    return pl.pallas_call(
        functools.partial(attend_kernel, pieces, first, early, final, unpack),
        out_shape=tuple(shapes),
        in_specs=specs,
        out_specs=tuple(out_specs),
        scratch_shapes=scratch,
        input_output_aliases=aliases,
        compiler_params=params(32),
        name="attend_late" if early else "attend",
    )(*operands)


def inverse(table):
    places = jnp.arange(table.shape[0], dtype=jnp.int32)
    return jnp.sum(jnp.where(table[None, :] == places[:, None], places, 0), axis=1)


def small_pieces(me, assignment, prefix_len, stripe_map, owner_map, queries, block_kv, table, pool):
    groups, slots, width = pool.shape
    count = block_kv.shape[0] // groups
    rot, bias, new_kv, _ = rotate_queries(
        None, me, assignment, prefix_len, stripe_map, queries, block_kv, table, groups * slots
    )
    spread = jnp.transpose(new_kv.reshape(count, groups, width), (1, 0, 2))
    fresh = spread[inverse(owner_map[assignment[me[0]]])]
    send = jnp.concatenate([pool[assignment], fresh], axis=1)
    got = lax.all_to_all(send, "pg", split_axis=0, concat_axis=0, tiled=True)
    keys = got[:, :slots].reshape(groups * slots, width)
    (attended,) = attend(rot, bias, new_kv, [keys])
    return attended, got[inverse(assignment), slots:]


def shards(queries, block_kv, pool_kv, prefix_len, assignment, stripe_map, owner_map):
    queries, block_kv, pool = queries[0], block_kv[0], pool_kv[0]
    groups, slots, _ = pool.shape
    new_count = queries.shape[0]
    count = new_count // groups
    me = lax.axis_index("pg").astype(jnp.int32).reshape(1)
    table = rotation_tables(new_count)
    if slots % 16 or count % 8 or slots % count or groups != 16:
        attended, decode_kv = small_pieces(
            me, assignment, prefix_len, stripe_map, owner_map, queries, block_kv, table, pool
        )
        return (attended[None], decode_kv[None])
    order = order_of(groups)
    blocks = front(order, me, assignment, prefix_len, owner_map, block_kv, table, pool)
    got = [blocks[0]]
    for p in range(1, groups):
        pairs = [(source, source ^ order[p]) for source in range(groups)]
        got.append(lax.ppermute(blocks[p], "pg", pairs))
    rot, bias, new_kv, requests = rotate_queries(
        order, me, assignment, prefix_len, stripe_map, queries, block_kv, table, groups * slots
    )
    soon = groups - LATE
    *sums, decode_kv = attend(rot, bias, new_kv, got[:soon], final=False, requests=requests)
    attended, decode_kv = attend(
        rot, bias, new_kv, got[soon:], first=soon, sums=sums, requests=requests, decode=decode_kv
    )
    return (attended[None], decode_kv[None])


def solution(mesh):
    return jax.shard_map(
        shards,
        mesh=mesh,
        in_specs=(
            P(("rep", "pg"), None, None),
            P(("rep", "pg"), None, None),
            P(("rep", "pg"), None, None, None),
            P("rep"),
            P("rep"),
            P("rep", None),
            P("rep", None),
        ),
        out_specs=(P(("rep", "pg"), None, None), P(("rep", "pg"), None, None, None)),
        check_vma=False,
    )
```

time: 49.7 us -> 45.5 us (0.915)
  the two profiles are of different devices: /device:TPU:19 before, /device:TPU:0 now
where the time goes in v4:
time: 45.5 us; the launch traced here: 45.2 us
  starting transfers between devices  25.4 us (56%)
  Pallas kernels  12.2 us (27%)
  local copies, waits for them, and re-layouts  4.75 us (10%)
  waiting for transfers between devices  2.05 us (5%)
  between operations  0.73 us (2%)
    ppermute x15, starting transfers between devices, shards(): got.append(lax.ppermute(blocks[p], 'pg', pairs))  25.4 us
    pallas_call x2, Pallas kernels, attend(): pl.pallas_call(functools.partial(attend_kernel, pieces, first, early, fin...  7.56 us
    unnamed x14, local copies, waits for them, and re-layouts  4.75 us
    pallas_call x1, Pallas kernels, front(): pl.pallas_call(functools.partial(front_kernel, order), out_shape=[block]...  3.23 us
    ppermute x15, waiting for transfers between devices, shards(): got.append(lax.ppermute(blocks[p], 'pg', pairs))  2.05 us
    pallas_call x1, Pallas kernels, rotate_queries(): pl.pallas_call(functools.partial(query_kernel, order), out_shape=(jax.Sha...  1.42 us
  transfers between devices with their start and end apart: 15, of which 3 were waited for; matrix products, arithmetic and copies ran while one was open for 0% of the time, Pallas kernels for 11%

profile of v4, /device:TPU:0, one launch (start us, length us, event | category | flops | bytes accessed | tf_op | source)
XLA Modules:
  0.0 45.2 jit_solution(4556385020106618627)
XLA Ops:
  0.6 3.2 %front.1 = (bf16[32,1280]{1,0:T(8,128)(2,1)}, bf16[32,1280]{1,0:T(8,128)(2,1)}, bf16[32,1280]{1,0:T(8,128)(2,1)}, bf16[32,1280]{1,0:T(8,128)(2,1)}, bf16[32,1280...) custom-call(s32[1]{0:T(128)} %bitcast.me_ref, ...), custom_call_target="tpu_custom_call" | custom-call | tf_op jit(solution)/shard_map/front/pallas_call | solution.py:125
  3.9 4.1 %collective-permute-start = (bf16[32,1280]{1,0:T(8,128)(2,1)}, bf16[32,1280]{1,0:T(8,128)(2,1)S(1)}, u32[]{:S(2)}, u32[]{:S(2)}) collective-permute-start(bf16[32,1280]{1,0:T(8,128)(2,1)} %get-tuple-element.32), channel_id=1, source_target_pairs={{0,8},{1,9},{2,10},{3,11},{4,12},{5,13},{6,14},{7,15},{8,0},{9,1},... | collective-permute-start | bytes 245768 | tf_op jit(solution)/shard_map/ppermute | solution.py:399
  8.0 1.7 %collective-permute-start.1 = (bf16[32,1280]{1,0:T(8,128)(2,1)}, bf16[32,1280]{1,0:T(8,128)(2,1)S(1)}, u32[]{:S(2)}, u32[]{:S(2)}) collective-permute-start(bf16[32,1280]{1,0:T(8,128)(2,1)} %get-tuple-element.33), channel_id=1, source_target_pairs={{0,7},{1,6},{2,5},{3,4},{4,3},{5,2},{6,1},{7,0},{8,15},{9,14},{10,... | collective-permute-start | bytes 245768 | tf_op jit(solution)/shard_map/ppermute | solution.py:399
  9.7 0.9 %collective-permute-start.2 = (bf16[32,1280]{1,0:T(8,128)(2,1)}, bf16[32,1280]{1,0:T(8,128)(2,1)S(1)}, u32[]{:S(2)}, u32[]{:S(2)}) collective-permute-start(bf16[32,1280]{1,0:T(8,128)(2,1)} %get-tuple-element.34), channel_id=1, source_target_pairs={{0,9},{1,8},{2,11},{3,10},{4,13},{5,12},{6,15},{7,14},{8,1},{9,0},... | collective-permute-start | bytes 245768 | tf_op jit(solution)/shard_map/ppermute | solution.py:399
  10.7 3.8 %collective-permute-start.4 = (bf16[32,1280]{1,0:T(8,128)(2,1)}, bf16[32,1280]{1,0:T(8,128)(2,1)S(1)}, u32[]{:S(2)}, u32[]{:S(2)}) collective-permute-start(bf16[32,1280]{1,0:T(8,128)(2,1)} %get-tuple-element.36), channel_id=1, source_target_pairs={{0,10},{1,11},{2,8},{3,9},{4,14},{5,15},{6,12},{7,13},{8,2},{9,3},... | collective-permute-start | bytes 245768 | tf_op jit(solution)/shard_map/ppermute | solution.py:399
  15.1 2.4 %collective-permute-start.6 = (bf16[32,1280]{1,0:T(8,128)(2,1)}, bf16[32,1280]{1,0:T(8,128)(2,1)S(1)}, u32[]{:S(2)}, u32[]{:S(2)}) collective-permute-start(bf16[32,1280]{1,0:T(8,128)(2,1)} %get-tuple-element.38), channel_id=1, source_target_pairs={{0,11},{1,10},{2,9},{3,8},{4,15},{5,14},{6,13},{7,12},{8,3},{9,2},... | collective-permute-start | bytes 245768 | tf_op jit(solution)/shard_map/ppermute | solution.py:399
  17.5 1.3 %collective-permute-start.7 = (bf16[32,1280]{1,0:T(8,128)(2,1)}, bf16[32,1280]{1,0:T(8,128)(2,1)S(1)}, u32[]{:S(2)}, u32[]{:S(2)}) collective-permute-start(bf16[32,1280]{1,0:T(8,128)(2,1)} %get-tuple-element.39), channel_id=1, source_target_pairs={{0,4},{1,5},{2,6},{3,7},{4,0},{5,1},{6,2},{7,3},{8,12},{9,13},{10,... | collective-permute-start | bytes 245768 | tf_op jit(solution)/shard_map/ppermute | solution.py:399
  18.8 1.4 %collective-permute-start.8 = (bf16[32,1280]{1,0:T(8,128)(2,1)}, bf16[32,1280]{1,0:T(8,128)(2,1)S(1)}, u32[]{:S(2)}, u32[]{:S(2)}) collective-permute-start(bf16[32,1280]{1,0:T(8,128)(2,1)} %get-tuple-element.40), channel_id=1, source_target_pairs={{0,12},{1,13},{2,14},{3,15},{4,8},{5,9},{6,10},{7,11},{8,4},{9,5},... | collective-permute-start | bytes 245768 | tf_op jit(solution)/shard_map/ppermute | solution.py:399
  20.2 1.0 %collective-permute-done.4.refs_8_ = bf16[32,1280]{1,0:T(8,128)(2,1)S(1)} collective-permute-done((bf16[32,1280]{1,0:T(8,128)(2,1)}, bf16[32,1280]{1,0:T(8,128)(2,1)S(1)}, u32[]{:S(2)}, u32[]{:S(2)}) %collective-permute-start.4) | collective-permute-done | bytes 81952 | tf_op jit(solution)/shard_map/ppermute | solution.py:399
  21.2 1.3 %collective-permute-start.9 = (bf16[32,1280]{1,0:T(8,128)(2,1)}, bf16[32,1280]{1,0:T(8,128)(2,1)S(1)}, u32[]{:S(2)}, u32[]{:S(2)}) collective-permute-start(bf16[32,1280]{1,0:T(8,128)(2,1)} %get-tuple-element.41), channel_id=1, source_target_pairs={{0,3},{1,2},{2,1},{3,0},{4,7},{5,6},{6,5},{7,4},{8,11},{9,10},{10,... | collective-permute-start | bytes 245768 | tf_op jit(solution)/shard_map/ppermute | solution.py:399
  22.5 1.9 %collective-permute-start.10 = (bf16[32,1280]{1,0:T(8,128)(2,1)}, bf16[32,1280]{1,0:T(8,128)(2,1)S(1)}, u32[]{:S(2)}, u32[]{:S(2)}) collective-permute-start(bf16[32,1280]{1,0:T(8,128)(2,1)} %get-tuple-element.42), channel_id=1, source_target_pairs={{0,13},{1,12},{2,15},{3,14},{4,9},{5,8},{6,11},{7,10},{8,5},{9,4},... | collective-permute-start | bytes 245768 | tf_op jit(solution)/shard_map/ppermute | solution.py:399
  24.4 1.5 %collective-permute-start.11 = (bf16[32,1280]{1,0:T(8,128)(2,1)}, bf16[32,1280]{1,0:T(8,128)(2,1)S(1)}, u32[]{:S(2)}, u32[]{:S(2)}) collective-permute-start(bf16[32,1280]{1,0:T(8,128)(2,1)} %get-tuple-element.47), channel_id=1, source_target_pairs={{0,2},{1,3},{2,0},{3,1},{4,6},{5,7},{6,4},{7,5},{8,10},{9,11},{10,... | collective-permute-start | bytes 245768 | tf_op jit(solution)/shard_map/ppermute | solution.py:399
  26.0 0.6 %collective-permute-done.7.refs_11_ = bf16[32,1280]{1,0:T(8,128)(2,1)S(1)} collective-permute-done((bf16[32,1280]{1,0:T(8,128)(2,1)}, bf16[32,1280]{1,0:T(8,128)(2,1)S(1)}, u32[]{:S(2)}, u32[]{:S(2)}) %collective-permute-start.7) | collective-permute-done | bytes 81952 | tf_op jit(solution)/shard_map/ppermute | solution.py:399
  26.5 2.1 %collective-permute-start.12 = (bf16[32,1280]{1,0:T(8,128)(2,1)}, bf16[32,1280]{1,0:T(8,128)(2,1)S(1)}, u32[]{:S(2)}, u32[]{:S(2)}) collective-permute-start(bf16[32,1280]{1,0:T(8,128)(2,1)} %get-tuple-element.48), channel_id=1, source_target_pairs={{0,14},{1,15},{2,12},{3,13},{4,10},{5,11},{6,8},{7,9},{8,6},{9,7},... | collective-permute-start | bytes 245768 | tf_op jit(solution)/shard_map/ppermute | solution.py:399
  28.7 2.7 %collective-permute-start.14 = (bf16[32,1280]{1,0:T(8,128)(2,1)}, bf16[32,1280]{1,0:T(8,128)(2,1)S(1)}, u32[]{:S(2)}, u32[]{:S(2)}) collective-permute-start(bf16[32,1280]{1,0:T(8,128)(2,1)} %get-tuple-element.50), channel_id=1, source_target_pairs={{0,15},{1,14},{2,13},{3,12},{4,11},{5,10},{6,9},{7,8},{8,7},{9,6},... | collective-permute-start | bytes 245768 | tf_op jit(solution)/shard_map/ppermute | solution.py:399
  31.4 0.9 %copy-done.1 = bf16[1,128,1024]{2,1,0:T(8,128)(2,1)S(1)} copy-done((bf16[1,128,1024]{2,1,0:T(8,128)(2,1)S(1)}, bf16[1,128,1024]{2,1,0:T(8,128)(2,1)}, u32[]{:S(2)}) %copy-start.1) | copy-done | bytes 262168
  32.3 0.9 %copy-done.2 = f32[264,128]{1,0:T(8,128)S(1)} copy-done((f32[264,128]{1,0:T(8,128)S(1)}, f32[264,128]{1,0:T(8,128)}, u32[]{:S(2)}) %copy-start.2) | copy-done | bytes 135192
  33.2 0.7 %copy-done.4 = s32[16,16]{1,0:T(8,128)S(1)} copy-done((s32[16,16]{1,0:T(8,128)S(1)}, s32[16,16]{1,0:T(8,128)}, u32[]{:S(2)}) %copy-start.4) | copy-done | bytes 1048
  33.9 0.7 %copy-done.5 = s32[16]{0:T(128)S(1)} copy-done((s32[16]{0:T(128)S(1)}, s32[16]{0:T(128)}, u32[]{:S(2)}) %copy-start.5) | copy-done | bytes 88
  34.6 0.7 %copy-done.6 = s32[16]{0:T(128)S(1)} copy-done((s32[16]{0:T(128)S(1)}, s32[16]{0:T(128)}, u32[]{:S(2)}) %copy-start.6) | copy-done | bytes 88
  35.2 1.4 %rotate_queries.1 = (bf16[4,1024,128]{2,1,0:T(8,128)(2,1)S(1)}, f32[8,512]{1,0:T(8,128)S(1)}, bf16[128,1024]{1,0:T(8,128)(2,1)S(1)}, s32[8,128]{1,0:T(8,128)S(1)}) custom-call(s32[1]{0:T(128)} %bitcast.me_ref, s32[16]{0:T(128)S(1)} %copy-done.5, s32[16]{0:T(128)S(1)} %copy-done.6, s32[16,16]{1,0:T(8,128)S(1)} %copy-done.4, bf16[128,4096]{1,0:T(8,128)(2,1)S(1)} %bitcast.6, ...), custom_call_target="tpu_custom_call" | custom-call | tf_op jit(solution)/shard_map/rotate_queries/pallas_call | solution.py:185
  36.7 0.9 %copy-done.3 = bf16[32,1280]{1,0:T(8,128)(2,1)S(1)} copy-done((bf16[32,1280]{1,0:T(8,128)(2,1)S(1)}, bf16[32,1280]{1,0:T(8,128)(2,1)}, u32[]{:S(2)}) %copy-start.3) | copy-done | bytes 81944
  37.6 3.8 %attend.1 = (f32[4,1024,128]{2,1,0:T(8,128)S(1)}, f32[4,1024,128]{2,1,0:T(8,128)S(1)}, f32[4,1024,128]{2,1,0:T(8,128)S(1)}, bf16[16,8,1024]{2,1,0:T(8,128)(2,1)}) custom-call(bf16[4,1024,128]{2,1,0:T(8,128)(2,1)S(1)} %get-tuple-element.28.refs_0_, f32[8,512]{1,0:T(8,128)S(1)} %get-tuple-element.29.refs_1_, bf16[128,1024]{1,0:T(8,128)(2,1)S(1)} %get-tuple-element.30.refs_2_, ...), custom_call_target="tpu_custom_call" | custom-call | tf_op jit(solution)/shard_map/attend/pallas_call | solution.py:350
  41.4 3.8 %attend_late.1 = (bf16[128,4096]{1,0:T(8,128)(2,1)}, bf16[16,8,1024]{2,1,0:T(8,128)(2,1)}) custom-call(bf16[4,1024,128]{2,1,0:T(8,128)(2,1)S(1)} %get-tuple-element.28.refs_0_, f32[8,512]{1,0:T(8,128)S(1)} %get-tuple-element.29.refs_1_, f32[4,1024,128]{2,1,0:T(8,128)S(1)} %get-tuple-element.44.refs_2_, ...), custom_call_target="tpu_custom_call", output_to_operand_aliasing={{1}: (10, {})} | custom-call | tf_op jit(solution)/shard_map/attend_late/pallas_call | solution.py:350
  (24 shorter events, 0.9 us)
Async XLA Ops:
  0.6 30.8 %copy-start = (bf16[1,128,4096]{2,1,0:T(8,128)(2,1)S(1)}, bf16[1,128,4096]{2,1,0:T(8,128)(2,1)}, u32[]{:S(2)}) copy-start(bf16[1,128,4096]{2,1,0:T(8,128)(2,1)} %param.8) | copy-start | bytes 3145732
  3.9 10.6 %collective-permute-start = (bf16[32,1280]{1,0:T(8,128)(2,1)}, bf16[32,1280]{1,0:T(8,128)(2,1)S(1)}, u32[]{:S(2)}, u32[]{:S(2)}) collective-permute-start(bf16[32,1280]{1,0:T(8,128)(2,1)} %get-tuple-element.32), channel_id=1, source_target_pairs={{0,8},{1,9},{2,10},{3,11},{4,12},{5,13},{6,14},{7,15},{8,0},{9,1},... | collective-permute-start | bytes 245768 | tf_op jit(solution)/shard_map/ppermute | solution.py:399
  8.0 7.1 %collective-permute-start.1 = (bf16[32,1280]{1,0:T(8,128)(2,1)}, bf16[32,1280]{1,0:T(8,128)(2,1)S(1)}, u32[]{:S(2)}, u32[]{:S(2)}) collective-permute-start(bf16[32,1280]{1,0:T(8,128)(2,1)} %get-tuple-element.33), channel_id=1, source_target_pairs={{0,7},{1,6},{2,5},{3,4},{4,3},{5,2},{6,1},{7,0},{8,15},{9,14},{10,... | collective-permute-start | bytes 245768 | tf_op jit(solution)/shard_map/ppermute | solution.py:399
  9.7 7.8 %collective-permute-start.2 = (bf16[32,1280]{1,0:T(8,128)(2,1)}, bf16[32,1280]{1,0:T(8,128)(2,1)S(1)}, u32[]{:S(2)}, u32[]{:S(2)}) collective-permute-start(bf16[32,1280]{1,0:T(8,128)(2,1)} %get-tuple-element.34), channel_id=1, source_target_pairs={{0,9},{1,8},{2,11},{3,10},{4,13},{5,12},{6,15},{7,14},{8,1},{9,0},... | collective-permute-start | bytes 245768 | tf_op jit(solution)/shard_map/ppermute | solution.py:399
  10.6 8.2 %collective-permute-start.3 = (bf16[32,1280]{1,0:T(8,128)(2,1)}, bf16[32,1280]{1,0:T(8,128)(2,1)S(1)}, u32[]{:S(2)}, u32[]{:S(2)}) collective-permute-start(bf16[32,1280]{1,0:T(8,128)(2,1)} %get-tuple-element.35), channel_id=1, source_target_pairs={{0,6},{1,7},{2,4},{3,5},{4,2},{5,3},{6,0},{7,1},{8,14},{9,15},{10,... | collective-permute-start | bytes 245768 | tf_op jit(solution)/shard_map/ppermute | solution.py:399
  10.7 10.5 %collective-permute-start.4 = (bf16[32,1280]{1,0:T(8,128)(2,1)}, bf16[32,1280]{1,0:T(8,128)(2,1)S(1)}, u32[]{:S(2)}, u32[]{:S(2)}) collective-permute-start(bf16[32,1280]{1,0:T(8,128)(2,1)} %get-tuple-element.36), channel_id=1, source_target_pairs={{0,10},{1,11},{2,8},{3,9},{4,14},{5,15},{6,12},{7,13},{8,2},{9,3},... | collective-permute-start | bytes 245768 | tf_op jit(solution)/shard_map/ppermute | solution.py:399
  14.5 8.0 %collective-permute-start.5 = (bf16[32,1280]{1,0:T(8,128)(2,1)}, bf16[32,1280]{1,0:T(8,128)(2,1)S(1)}, u32[]{:S(2)}, u32[]{:S(2)}) collective-permute-start(bf16[32,1280]{1,0:T(8,128)(2,1)} %get-tuple-element.37), channel_id=1, source_target_pairs={{0,5},{1,4},{2,7},{3,6},{4,1},{5,0},{6,3},{7,2},{8,13},{9,12},{10,... | collective-permute-start | bytes 245768 | tf_op jit(solution)/shard_map/ppermute | solution.py:399
  15.1 9.3 %collective-permute-start.6 = (bf16[32,1280]{1,0:T(8,128)(2,1)}, bf16[32,1280]{1,0:T(8,128)(2,1)S(1)}, u32[]{:S(2)}, u32[]{:S(2)}) collective-permute-start(bf16[32,1280]{1,0:T(8,128)(2,1)} %get-tuple-element.38), channel_id=1, source_target_pairs={{0,11},{1,10},{2,9},{3,8},{4,15},{5,14},{6,13},{7,12},{8,3},{9,2},... | collective-permute-start | bytes 245768 | tf_op jit(solution)/shard_map/ppermute | solution.py:399
  17.5 9.0 %collective-permute-start.7 = (bf16[32,1280]{1,0:T(8,128)(2,1)}, bf16[32,1280]{1,0:T(8,128)(2,1)S(1)}, u32[]{:S(2)}, u32[]{:S(2)}) collective-permute-start(bf16[32,1280]{1,0:T(8,128)(2,1)} %get-tuple-element.39), channel_id=1, source_target_pairs={{0,4},{1,5},{2,6},{3,7},{4,0},{5,1},{6,2},{7,3},{8,12},{9,13},{10,... | collective-permute-start | bytes 245768 | tf_op jit(solution)/shard_map/ppermute | solution.py:399
  18.8 9.8 %collective-permute-start.8 = (bf16[32,1280]{1,0:T(8,128)(2,1)}, bf16[32,1280]{1,0:T(8,128)(2,1)S(1)}, u32[]{:S(2)}, u32[]{:S(2)}) collective-permute-start(bf16[32,1280]{1,0:T(8,128)(2,1)} %get-tuple-element.40), channel_id=1, source_target_pairs={{0,12},{1,13},{2,14},{3,15},{4,8},{5,9},{6,10},{7,11},{8,4},{9,5},... | collective-permute-start | bytes 245768 | tf_op jit(solution)/shard_map/ppermute | solution.py:399
  21.2 7.5 %collective-permute-start.9 = (bf16[32,1280]{1,0:T(8,128)(2,1)}, bf16[32,1280]{1,0:T(8,128)(2,1)S(1)}, u32[]{:S(2)}, u32[]{:S(2)}) collective-permute-start(bf16[32,1280]{1,0:T(8,128)(2,1)} %get-tuple-element.41), channel_id=1, source_target_pairs={{0,3},{1,2},{2,1},{3,0},{4,7},{5,6},{6,5},{7,4},{8,11},{9,10},{10,... | collective-permute-start | bytes 245768 | tf_op jit(solution)/shard_map/ppermute | solution.py:399
  22.5 14.1 %collective-permute-start.10 = (bf16[32,1280]{1,0:T(8,128)(2,1)}, bf16[32,1280]{1,0:T(8,128)(2,1)S(1)}, u32[]{:S(2)}, u32[]{:S(2)}) collective-permute-start(bf16[32,1280]{1,0:T(8,128)(2,1)} %get-tuple-element.42), channel_id=1, source_target_pairs={{0,13},{1,12},{2,15},{3,14},{4,9},{5,8},{6,11},{7,10},{8,5},{9,4},... | collective-permute-start | bytes 245768 | tf_op jit(solution)/shard_map/ppermute | solution.py:399
  24.4 16.9 %collective-permute-start.11 = (bf16[32,1280]{1,0:T(8,128)(2,1)}, bf16[32,1280]{1,0:T(8,128)(2,1)S(1)}, u32[]{:S(2)}, u32[]{:S(2)}) collective-permute-start(bf16[32,1280]{1,0:T(8,128)(2,1)} %get-tuple-element.47), channel_id=1, source_target_pairs={{0,2},{1,3},{2,0},{3,1},{4,6},{5,7},{6,4},{7,5},{8,10},{9,11},{10,... | collective-permute-start | bytes 245768 | tf_op jit(solution)/shard_map/ppermute | solution.py:399
  26.5 14.8 %collective-permute-start.12 = (bf16[32,1280]{1,0:T(8,128)(2,1)}, bf16[32,1280]{1,0:T(8,128)(2,1)S(1)}, u32[]{:S(2)}, u32[]{:S(2)}) collective-permute-start(bf16[32,1280]{1,0:T(8,128)(2,1)} %get-tuple-element.48), channel_id=1, source_target_pairs={{0,14},{1,15},{2,12},{3,13},{4,10},{5,11},{6,8},{7,9},{8,6},{9,7},... | collective-permute-start | bytes 245768 | tf_op jit(solution)/shard_map/ppermute | solution.py:399
  28.6 12.7 %collective-permute-start.13 = (bf16[32,1280]{1,0:T(8,128)(2,1)}, bf16[32,1280]{1,0:T(8,128)(2,1)S(1)}, u32[]{:S(2)}, u32[]{:S(2)}) collective-permute-start(bf16[32,1280]{1,0:T(8,128)(2,1)} %get-tuple-element.49), channel_id=1, source_target_pairs={{0,1},{1,0},{2,3},{3,2},{4,5},{5,4},{6,7},{7,6},{8,9},{9,8},{10,11... | collective-permute-start | bytes 245768 | tf_op jit(solution)/shard_map/ppermute | solution.py:399
  28.7 12.7 %collective-permute-start.14 = (bf16[32,1280]{1,0:T(8,128)(2,1)}, bf16[32,1280]{1,0:T(8,128)(2,1)S(1)}, u32[]{:S(2)}, u32[]{:S(2)}) collective-permute-start(bf16[32,1280]{1,0:T(8,128)(2,1)} %get-tuple-element.50), channel_id=1, source_target_pairs={{0,15},{1,14},{2,13},{3,12},{4,11},{5,10},{6,9},{7,8},{8,7},{9,6},... | collective-permute-start | bytes 245768 | tf_op jit(solution)/shard_map/ppermute | solution.py:399
  31.4 1.0 %copy-start.1 = (bf16[1,128,1024]{2,1,0:T(8,128)(2,1)S(1)}, bf16[1,128,1024]{2,1,0:T(8,128)(2,1)}, u32[]{:S(2)}) copy-start(bf16[1,128,1024]{2,1,0:T(8,128)(2,1)} %param.9) | copy-start | bytes 786436
  32.3 0.9 %copy-start.2 = (f32[264,128]{1,0:T(8,128)S(1)}, f32[264,128]{1,0:T(8,128)}, u32[]{:S(2)}) copy-start(f32[264,128]{1,0:T(8,128)} %constant.6.clone.table_ref.table_any) | copy-start | bytes 405508
  33.2 0.7 %copy-start.4 = (s32[16,16]{1,0:T(8,128)S(1)}, s32[16,16]{1,0:T(8,128)}, u32[]{:S(2)}) copy-start(s32[16,16]{1,0:T(8,128)} %stripe_ref.1) | copy-start | bytes 3076
  33.9 0.7 %copy-start.5 = (s32[16]{0:T(128)S(1)}, s32[16]{0:T(128)}, u32[]{:S(2)}) copy-start(s32[16]{0:T(128)} %assign_any.1) | copy-start | bytes 196
  34.6 0.7 %copy-start.6 = (s32[16]{0:T(128)S(1)}, s32[16]{0:T(128)}, u32[]{:S(2)}) copy-start(s32[16]{0:T(128)} %length_any.1) | copy-start | bytes 196
  36.7 0.9 %copy-start.3 = (bf16[32,1280]{1,0:T(8,128)(2,1)S(1)}, bf16[32,1280]{1,0:T(8,128)(2,1)}, u32[]{:S(2)}) copy-start(bf16[32,1280]{1,0:T(8,128)(2,1)} %get-tuple-element.31.refs_3_) | copy-start | bytes 245764
